TPU v7x, 128 devices: a whole 4x4x4 slice. The times are simulated.
128 devices in a mesh: section: 4 (over x), expert: 32 (over z, y, core).
Axes of the slice: x: 4, y: 4, z: 4, core: 2. Of those that a mesh axis runs over, the one named last changes fastest.
Arguments:
- stash: bfloat16 [4, 4096, 4096], P('section', 'expert'), may hold values from -6 to 6
- out_grad: bfloat16 [4, 4096, 4096], P('section', 'expert'), may hold values from -6 to 6
- expert_ids: int32 [4, 4096, 1], P('section', 'expert'), may hold values from 0 to 7; in each aligned block of 128 rows (0 to 127, 128 to 255, ..., all dimensions but the last counted through in order) at most 24 rows name the same one
- gate_probs: float32 [4, 4096, 1], P('section', 'expert'), may hold values from 0.05 to 1
- w_gate: bfloat16 [4, 32, 4096, 384], P('section', 'expert'), may hold values from -0.09375 to 0.09375
- w_up: bfloat16 [4, 32, 4096, 384], P('section', 'expert'), may hold values from -0.09375 to 0.09375
- w_down: bfloat16 [4, 32, 384, 4096], P('section', 'expert'), may hold values from -0.15625 to 0.15625
Outputs:
- prev_grad: bfloat16 [4, 4096, 4096], P('section', 'expert')
- grad_gate: bfloat16 [4, 32, 4096, 384], P('section', 'expert')
- grad_up: bfloat16 [4, 32, 4096, 384], P('section', 'expert')
- grad_down: bfloat16 [4, 32, 384, 4096], P('section', 'expert')
Inputs may be any that keep to these rules, and one draw needn't show every extreme that they name: `expert_ids`: among the 128 tokens of one device (aligned blocks of rows of one layer), no expert is named more than 24 times; in every draw some expert is named exactly 24 times by the tokens of some device. Each token chooses exactly one expert.
All inputs are finite; a program needn't handle non-finite values.
Results may differ from a plain program's by a relative error of at most 0.0058.
Values may be sent and summed in bfloat16 or wider, within the bound.
No kernel may reach another device: no remote copies, remote signals or barrier semaphores. Data moves between devices by JAX's collectives and lax.ppermute only.
A program may use at most 192 MiB of HBM per device.

v0:
```python
import jax
import jax.numpy as jnp
from jax import lax
from jax.sharding import PartitionSpec as P

SPLIT = 4


def shifted(value, axis, by):
    length = lax.axis_size(axis)
    return lax.ppermute(value, axis, [(i, (i + by) % length) for i in range(length)])


def contract(left, right, left_dim, right_dim):
    return lax.dot_general(
        left, right, (((left_dim,), (right_dim,)), ((), ())), preferred_element_type=jnp.float32
    )


def expert_grads(token_rows, grad_rows, gate_weight, up_weight, down_weight):
    gate_pre = contract(token_rows, gate_weight, 1, 0)
    up_pre = contract(token_rows, up_weight, 1, 0)
    sigmoid_a = jax.nn.sigmoid(gate_pre)
    silu_a = gate_pre * sigmoid_a
    hidden = (silu_a * up_pre).astype(jnp.bfloat16)
    grad_down = contract(hidden, grad_rows, 0, 0).astype(jnp.bfloat16)
    hidden_grad = contract(grad_rows, down_weight, 1, 1)
    gate_delta = (hidden_grad * up_pre * sigmoid_a * (1.0 + gate_pre * (1.0 - sigmoid_a))).astype(
        jnp.bfloat16
    )
    up_delta = (hidden_grad * silu_a).astype(jnp.bfloat16)
    grad_gate = contract(token_rows, gate_delta, 0, 0).astype(jnp.bfloat16)
    grad_up = contract(token_rows, up_delta, 0, 0).astype(jnp.bfloat16)
    row_grads = contract(gate_delta, gate_weight, 1, 1) + contract(up_delta, up_weight, 1, 1)
    return (row_grads, grad_gate, grad_up, grad_down)


def body(stash, out_grad, expert_ids, gate_probs, w_gate, w_up, w_down):
    device_count = lax.axis_size("expert")
    token_count = expert_ids.shape[1]
    top_count = expert_ids.shape[2]
    model_width = stash.shape[2]
    expert_count = device_count // SPLIT
    capacity = token_count * top_count * 3 // (2 * expert_count)
    routed = expert_ids[0].reshape(-1)
    onehot = (routed[:, None] == jnp.arange(expert_count, dtype=jnp.int32)[None, :]).astype(
        jnp.int32
    )
    slot_rank = jnp.sum((jnp.cumsum(onehot, axis=0) - onehot) * onehot, axis=1)
    slot_index = routed * capacity + slot_rank
    scaled = (gate_probs[0][:, :, None] * out_grad[0][:, None, :].astype(jnp.float32)).astype(
        jnp.bfloat16
    )
    token_rows = jnp.repeat(stash[0], top_count, axis=0)
    paired = jnp.concatenate(
        [token_rows, scaled.reshape(token_count * top_count, model_width)], axis=1
    )
    outgoing = (
        jnp.zeros((expert_count * capacity, 2 * model_width), jnp.bfloat16)
        .at[slot_index]
        .set(paired)
    )
    copies = jnp.broadcast_to(
        outgoing.reshape(expert_count, 1, capacity, 2 * model_width),
        (expert_count, SPLIT, capacity, 2 * model_width),
    )
    incoming = lax.all_to_all(
        copies.reshape(device_count, capacity, 2 * model_width),
        "expert",
        split_axis=0,
        concat_axis=0,
        tiled=True,
    )
    flat_rows = incoming.reshape(device_count * capacity, 2 * model_width)
    row_grads, grad_gate, grad_up, grad_down = expert_grads(
        flat_rows[:, :model_width],
        flat_rows[:, model_width:],
        w_gate[0, 0],
        w_up[0, 0],
        w_down[0, 0],
    )
    returned = lax.all_to_all(
        row_grads.reshape(device_count, capacity, model_width),
        "expert",
        split_axis=0,
        concat_axis=0,
        tiled=True,
    )
    summed = jnp.sum(returned.reshape(expert_count, SPLIT, capacity, model_width), axis=1)
    pair_grads = summed.reshape(expert_count * capacity, model_width)[slot_index]
    input_grad = jnp.sum(pair_grads.reshape(token_count, top_count, model_width), axis=1).astype(
        jnp.bfloat16
    )
    prev_grad = shifted(input_grad[None], "section", -1)
    return (prev_grad, grad_gate[None, None], grad_up[None, None], grad_down[None, None])


def solution(mesh):
    placed = (
        P("section", "expert", None),
        P("section", "expert", None),
        P("section", "expert", None),
        P("section", "expert", None),
        P("section", "expert", None, None),
        P("section", "expert", None, None),
        P("section", "expert", None, None),
    )
    return jax.shard_map(
        body,
        mesh=mesh,
        in_specs=placed,
        out_specs=(
            P("section", "expert", None),
            P("section", "expert", None, None),
            P("section", "expert", None, None),
            P("section", "expert", None, None),
        ),
        check_vma=False,
    )
```

profile of v0, /device:TPU:6, one launch (start us, length us, event | category | flops | bytes accessed | tf_op | source)
XLA Modules:
  0.0 384.7 jit_solution(18386042479667617270)
XLA Ops:
  0.6 0.0 copy-start
  0.6 0.9 fusion.28
  1.5 0.2 reduce_window_sum.11
  1.7 0.8 select_reduce_fusion
  2.5 0.7 fusion.29
  3.2 2.5 fusion.24
  5.7 6.4 %scatter_custom_fusion = bf16[192,8192]{1,0:T(8,128)(2,1)} fusion(s32[128]{0:T(128)S(1)} %fusion.29, bf16[128,4096]{1,0:T(8,128)(2,1)} %fusion.24, bf16[]{:T(256)} %constant.24, bf16[128,4096]{1,0:T(8,128)(2,1)} %bitcast.60, bf16[]{:T(256)} %constant.6.clone.1), kind=kCustom, calls=%fused_computation.25 | custom fusion | flops 4194304 | bytes 5242884 | tf_op jit(solution)/shard_map/scatter | solution.py:61
  12.1 8.0 %broadcast_in_dim.25 = bf16[8,4,24,8192]{3,2,1,0:T(8,128)(2,1)} broadcast(bf16[8,24,8192]{2,1,0:T(8,128)(2,1)} %bitcast.59), dimensions={0,2,3} | broadcast | bytes 15728640 | tf_op jit(solution)/shard_map/broadcast_in_dim | solution.py:63
  20.1 149.3 %all_to_all.10 = bf16[32,24,8192]{2,1,0:T(8,128)(2,1)S(1)} all-to-all(bf16[32,24,8192]{2,1,0:T(8,128)(2,1)} %bitcast.52), channel_id=1, replica_groups=mesh['section'=4,'expert'=32] {'expert'}, dimensions={0} | all-to-all | bytes 25165824 | tf_op jit(solution)/shard_map/all_to_all | solution.py:67
  169.3 0.0 copy-start.2
  169.3 0.0 copy-done
  169.3 0.0 copy-start.3
  169.4 3.4 fusion.10
  172.8 0.8 copy-done.3
  173.6 0.0 copy-start.9
  173.6 0.0 copy-start.8
  173.6 3.4 fusion.12
  177.0 0.0 copy-done.2
  177.0 0.0 copy-done.9
  177.0 0.0 copy-done.8
  177.0 0.0 copy-start.11
  177.1 3.8 multiply_convert_fusion.1
  180.8 0.0 copy-done.11
  180.8 0.0 copy-start.6
  180.9 0.0 copy-start.4
  180.9 3.5 fusion.14
  184.3 0.0 copy-done.6
  184.3 0.0 copy-done.4
  184.3 6.6 %convolution_add_fusion = f32[768,4096]{1,0:T(8,128)} fusion(f32[768,4096]{1,0:T(8,128)S(1)} %fusion.14, bf16[768,384]{1,0:T(8,128)(2,1)S(1)} %get-tuple-element.4, bf16[1,1,4096,384]{3,2,1,0:T(8,128)(2,1)S(1)} %copy-done.3), kind=kOutput, calls=%fused_computation.3 | convolution fusion | flops 2419064832 | bytes 28901376 | tf_op jit(solution)/shard_map/dot_general | solution.py:15
  191.0 0.0 copy-start.5
  191.0 6.4 %all-to-all-start.1 = ((f32[32,24,4096]{2,1,0:T(8,128)}), f32[32,24,4096]{2,1,0:T(8,128)}, u32[]{:S(2)}, u32[]{:S(2)}) async-start(f32[32,24,4096]{2,1,0:T(8,128)} %bitcast.50), calls=%async_computation.1 | async-start | bytes 25165824 | tf_op jit(solution)/shard_map/all_to_all | solution.py:82
  197.4 0.0 copy-done.5
  197.4 7.9 %fusion.4 = bf16[1,1,4096,384]{3,2,1,0:T(8,128)(2,1)} fusion(bf16[768,384]{1,0:T(8,128)(2,1)S(1)} %copy-done.5, bf16[768,8192]{1,0:T(8,128)(2,1)} %bitcast.56), kind=kOutput, calls=%fused_computation.11 | convolution fusion | flops 2417491968 | bytes 10027008 | tf_op jit(solution)/shard_map/dot_general | solution.py:15
  205.3 152.7 %all-to-all-done.1 = f32[32,24,4096]{2,1,0:T(8,128)} async-done(((f32[32,24,4096]{2,1,0:T(8,128)}), f32[32,24,4096]{2,1,0:T(8,128)}, u32[]{:S(2)}, u32[]{:S(2)}) %all-to-all-start.1) | async-done | bytes 12582944 | tf_op jit(solution)/shard_map/all_to_all | solution.py:82
  358.0 6.2 %bitcast_reduce_fusion = bf16[8,24,4096]{2,1,0:T(8,128)(2,1)S(1)} fusion(f32[32,24,4096]{2,1,0:T(8,128)} %all-to-all-done.1), kind=kLoop, calls=%fused_computation.2 | loop fusion | flops 2359296 | bytes 14155776 | tf_op jit(solution)/shard_map/reduce_sum | solution.py:89
  364.2 0.0 copy-start.7
  364.2 2.2 gather_fusion
  366.4 0.0 copy-start.10
  366.4 0.0 copy-start.12
  366.4 0.8 collective-permute-start
  367.2 0.0 copy-done.7
  367.2 7.9 %fusion.3 = bf16[1,1,4096,384]{3,2,1,0:T(8,128)(2,1)} fusion(bf16[768,384]{1,0:T(8,128)(2,1)S(1)} %copy-done.7, bf16[768,8192]{1,0:T(8,128)(2,1)} %bitcast.57), kind=kOutput, calls=%fused_computation.10 | convolution fusion | flops 2417491968 | bytes 10027008 | tf_op jit(solution)/shard_map/dot_general | solution.py:15
  375.1 0.0 copy-done.10
  375.1 0.0 copy-done.12
  375.2 7.4 %fusion.5 = bf16[1,1,384,4096]{3,2,1,0:T(8,128)(2,1)} fusion(bf16[768,8192]{1,0:T(8,128)(2,1)} %bitcast.58, f32[768,384]{1,0:T(8,128)S(1)} %copy-done.12, f32[768,384]{1,0:T(8,128)S(1)} %copy-done.10), kind=kOutput, calls=%fused_computation.12 | convolution fusion | flops 2419261440 | bytes 11796480 | tf_op jit(solution)/shard_map/dot_general | solution.py:15
  382.5 1.3 collective-permute-done
  383.8 1.0 copy.12
  384.7 0.0 copy-done.1
  (2 shorter events, 0.0 us)
Async XLA Ops:
  0.6 168.7 %copy-start = (bf16[1,1,4096,384]{3,2,1,0:T(8,128)(2,1)S(1)}, bf16[1,1,4096,384]{3,2,1,0:T(8,128)(2,1)}, u32[]{:S(2)}) copy-start(bf16[1,1,4096,384]{3,2,1,0:T(8,128)(2,1)} %param.11) | copy-start | bytes 9437188
  169.3 7.7 %copy-start.2 = (bf16[32,24,8192]{2,1,0:T(8,128)(2,1)}, bf16[32,24,8192]{2,1,0:T(8,128)(2,1)S(1)}, u32[]{:S(2)}) copy-start(bf16[32,24,8192]{2,1,0:T(8,128)(2,1)S(1)} %all_to_all.10) | copy-start | bytes 37748740
  169.3 4.2 %copy-start.3 = (bf16[1,1,4096,384]{3,2,1,0:T(8,128)(2,1)S(1)}, bf16[1,1,4096,384]{3,2,1,0:T(8,128)(2,1)}, u32[]{:S(2)}) copy-start(bf16[1,1,4096,384]{3,2,1,0:T(8,128)(2,1)} %param.12) | copy-start | bytes 9437188
  173.6 3.4 copy-start.9
  173.6 3.5 copy-start.8
  177.0 3.8 copy-start.11
  180.8 3.5 copy-start.6
  180.9 3.5 copy-start.4
  191.0 6.5 %copy-start.5 = (bf16[768,384]{1,0:T(8,128)(2,1)S(1)}, bf16[768,384]{1,0:T(8,128)(2,1)}, u32[]{:S(2)}) copy-start(bf16[768,384]{1,0:T(8,128)(2,1)} %copy-done.4) | copy-start | bytes 1769476
  191.0 167.1 %all-to-all-start.1 = ((f32[32,24,4096]{2,1,0:T(8,128)}), f32[32,24,4096]{2,1,0:T(8,128)}, u32[]{:S(2)}, u32[]{:S(2)}) async-start(f32[32,24,4096]{2,1,0:T(8,128)} %bitcast.50), calls=%async_computation.1 | async-start | bytes 25165824 | tf_op jit(solution)/shard_map/all_to_all | solution.py:82
  364.2 3.0 copy-start.7
  366.4 8.8 %copy-start.10 = (f32[768,384]{1,0:T(8,128)S(1)}, f32[768,384]{1,0:T(8,128)}, u32[]{:S(2)}) copy-start(f32[768,384]{1,0:T(8,128)} %copy-done.9) | copy-start | bytes 3538948
  366.4 8.8 %copy-start.12 = (f32[768,384]{1,0:T(8,128)S(1)}, f32[768,384]{1,0:T(8,128)}, u32[]{:S(2)}) copy-start(f32[768,384]{1,0:T(8,128)} %copy-done.11) | copy-start | bytes 3538948
  366.4 17.4 %collective-permute-start = (bf16[1,128,4096]{2,1,0:T(8,128)(2,1)}, bf16[1,128,4096]{2,1,0:T(8,128)(2,1)S(1)}, u32[]{:S(2)}, u32[]{:S(2)}) collective-permute-start(bf16[1,128,4096]{2,1,0:T(8,128)(2,1)} %bitcast.42), channel_id=1, source_target_pairs={{0,96},{32,0},{64,32},{96,64},{1,97},{33,1},{65,33},{97,65},{2,98}... | collective-permute-start | bytes 3145736 | tf_op jit(solution)/shard_map/ppermute | solution.py:11
  375.1 9.6 %copy-start.1 = (bf16[1,1,4096,384]{3,2,1,0:T(8,128)(2,1)S(1)}, bf16[1,1,4096,384]{3,2,1,0:T(8,128)(2,1)}, u32[]{:S(2)}) copy-start(bf16[1,1,4096,384]{3,2,1,0:T(8,128)(2,1)} %param.11) | copy-start | bytes 9437188
where the time goes:
time: 388 us; the launch traced here: 385 us
  waiting for transfers between devices  154 us (40%)
  blocking collectives  149 us (38%)
  matrix products  43.9 us (11%)
  other arithmetic  17.6 us (5%)
  local copies, waits for them, and re-layouts  12 us (3%)
  starting transfers between devices  7.25 us (2%)
    all_to_all x1, waiting for transfers between devices, body(): lax.all_to_all(row_grads.reshape(device_count, capacity, model_width), 'e...  153 us
    all_to_all x1, blocking collectives, body(): lax.all_to_all(copies.reshape(device_count, capacity, 2 * model_width), '...  149 us
    dot_general x8, matrix products, contract(): lax.dot_general(left, right, (((left_dim,), (right_dim,)), ((), ())), pre...  43.9 us
    broadcast_in_dim x1, local copies, waits for them, and re-layouts, body(): jnp.broadcast_to(outgoing.reshape(expert_count, 1, capacity, 2 * model_wi...  7.98 us
  transfers between devices with their start and end apart: 2, of which 2 were waited for; matrix products, arithmetic and copies ran while one was open for 6% of the time, Pallas kernels for 0%

commit v1 on v0

v1 whole, which is shorter than its diff:
```python
import jax
import jax.numpy as jnp
import numpy as np
from jax import lax
from jax.sharding import Mesh, PartitionSpec as P

SPLIT = 4
CORES = 2


def contract(left, right, left_dim, right_dim):
    return lax.dot_general(
        left, right, (((left_dim,), (right_dim,)), ((), ())), preferred_element_type=jnp.float32
    )


def swap_cores(value):
    return lax.ppermute(value, "core", [(0, 1), (1, 0)])


def over_chips(value):
    return lax.all_to_all(value, "chip", split_axis=0, concat_axis=0, tiled=True)


def body(stash, out_grad, expert_ids, gate_probs, w_gate, w_up, w_down):
    chips = lax.axis_size("chip")
    sections = lax.axis_size("section")
    tokens, width = stash.shape[1], stash.shape[2]
    experts = chips * CORES // SPLIT
    halves = SPLIT // CORES
    capacity = tokens * 3 // (2 * experts)
    slots = experts * capacity
    routed = expert_ids[0].reshape(-1)
    onehot = (routed[:, None] == jnp.arange(experts, dtype=jnp.int32)[None, :]).astype(jnp.int32)
    rank = jnp.sum((jnp.cumsum(onehot, axis=0) - onehot) * onehot, axis=1)
    slot = routed * capacity + rank
    place = (jnp.arange(slots, dtype=jnp.int32)[:, None] == slot[None, :]).astype(jnp.bfloat16)
    scaled = (gate_probs[0] * out_grad[0].astype(jnp.float32)).astype(jnp.bfloat16)

    def deal(rows):
        packed = contract(place, rows, 1, 0).astype(jnp.bfloat16)
        packed = packed.reshape(experts, 1, capacity, width)
        copies = jnp.broadcast_to(packed, (experts, halves, capacity, width))
        return copies.reshape(chips, capacity, width)

    mine = over_chips(jnp.concatenate([deal(stash[0]), deal(scaled)], axis=2))
    other = swap_cores(mine)
    rows = chips * capacity
    both = jnp.concatenate([mine, other], axis=0).reshape(2 * rows, 2 * width)
    token_rows, grad_rows = both[:, :width], both[:, width:]
    wg, wu, wd = w_gate[0, 0], w_up[0, 0], w_down[0, 0]
    gate_pre = contract(token_rows, wg, 1, 0)
    up_pre = contract(token_rows, wu, 1, 0)
    sigmoid_a = jax.nn.sigmoid(gate_pre)
    silu_a = gate_pre * sigmoid_a
    hidden = (silu_a * up_pre).astype(jnp.bfloat16)
    hidden_grad = contract(grad_rows, wd, 1, 1)
    gate_delta = (hidden_grad * up_pre * sigmoid_a * (1.0 + gate_pre * (1.0 - sigmoid_a))).astype(
        jnp.bfloat16
    )
    up_delta = (hidden_grad * silu_a).astype(jnp.bfloat16)
    row_grads = contract(gate_delta, wg, 1, 1) + contract(up_delta, wu, 1, 1)
    theirs = swap_cores(row_grads[rows:].astype(jnp.bfloat16))
    back = (row_grads[:rows] + theirs.astype(jnp.float32)).astype(jnp.bfloat16)
    returned = over_chips(back.reshape(chips, capacity, width))
    returned = returned.reshape(experts, halves, capacity, width)
    place_back = jnp.broadcast_to(
        place.reshape(experts, 1, capacity, tokens), (experts, halves, capacity, tokens)
    ).reshape(experts * halves * capacity, tokens)
    input_grad = contract(
        place_back, returned.reshape(experts * halves * capacity, width), 0, 0
    ).astype(jnp.bfloat16)
    prev_grad = lax.ppermute(
        input_grad, "section", [(i, (i - 1) % sections) for i in range(sections)]
    )
    grad_down = contract(hidden, grad_rows, 0, 0).astype(jnp.bfloat16)
    grad_gate = contract(token_rows, gate_delta, 0, 0).astype(jnp.bfloat16)
    grad_up = contract(token_rows, up_delta, 0, 0).astype(jnp.bfloat16)
    return (prev_grad[None], grad_gate[None, None], grad_up[None, None], grad_down[None, None])


def solution(mesh):
    sections, devices = mesh.devices.shape
    fine = Mesh(mesh.devices.reshape(sections, devices // CORES, CORES), ("section", "chip", "core"))
    spec = P("section", ("chip", "core"))
    return jax.shard_map(
        body, mesh=fine, in_specs=(spec,) * 7, out_specs=(spec,) * 4, check_vma=False
    )
```

time: 388 us -> 221 us (0.57)
  waiting for transfers between devices: 154 us -> 68.4 us
  blocking collectives: 149 us -> 81.2 us
  other arithmetic: 17.6 us -> 11.9 us
  local copies, waits for them, and re-layouts: 12 us -> 7.53 us
    all_to_all x1, waiting for transfers between devices: 153 us -> 40.9 us  [over_chips(): lax.all_to_all(value, 'chip', split_axis=0, concat_axis=0, tiled=True)]
    all_to_all x1, blocking collectives: 149 us -> 81.2 us  [over_chips(): lax.all_to_all(value, 'chip', split_axis=0, concat_axis=0, tiled=True)]
    ppermute x1 -> x3, waiting for transfers between devices: 1.26 us -> 27.5 us  [the longest x2 15.7 us: swap_cores(): return lax.ppermute(value, 'core', [(0, 1), (1, 0)])]
    scatter x1 -> x0, other arithmetic: 6.42 us -> none  [body(): outgoing = jnp.zeros((expert_count * capacity, 2 * model_width), jnp.bflo...]
    reduce_sum x2 -> x1, other arithmetic: 7.02 us -> 0.91 us  [body(): rank = jnp.sum((jnp.cumsum(onehot, axis=0) - onehot) * onehot, axis=1)]
    broadcast_in_dim x1 -> x3, local copies, waits for them, and re-layouts: 7.98 us -> 2.43 us  [the longest x2 2.42 us: deal(): copies = jnp.broadcast_to(packed, (experts, halves, capacity, width))]
    dot_general x8 -> x11, matrix products: 43.9 us -> 45.1 us  [contract(): lax.dot_general(left, right, (((left_dim,), (right_dim,)), ((), ())), pre...]
  transfers between devices with their start and end apart: 2 -> 4, of which waited for: 2 -> 4; matrix products, arithmetic and copies ran while one was open for 6% -> 10% of each run, Pallas kernels for 0% -> 0%
where the time goes in v1:
time: 221 us; the launch traced here: 220 us
  blocking collectives  81.2 us (37%)
  waiting for transfers between devices  68.4 us (31%)
  matrix products  45.1 us (20%)
  other arithmetic  11.9 us (5%)
  local copies, waits for them, and re-layouts  7.53 us (3%)
  starting transfers between devices  5.08 us (2%)
    all_to_all x1, blocking collectives, over_chips(): lax.all_to_all(value, 'chip', split_axis=0, concat_axis=0, tiled=True)  81.2 us
    dot_general x11, matrix products, contract(): lax.dot_general(left, right, (((left_dim,), (right_dim,)), ((), ())), pre...  45.1 us
    all_to_all x1, waiting for transfers between devices, over_chips(): lax.all_to_all(value, 'chip', split_axis=0, concat_axis=0, tiled=True)  40.9 us
    ppermute x2, waiting for transfers between devices, swap_cores(): return lax.ppermute(value, 'core', [(0, 1), (1, 0)])  15.7 us
    ppermute x1, waiting for transfers between devices, body(): lax.ppermute(input_grad, 'section', [(i, (i - 1) % sections) for i in ran...  11.8 us
    convert_element_type x1, other arithmetic, body(): back = (row_grads[:rows] + theirs.astype(jnp.float32)).astype(jnp.bfloat16)  5.41 us
  transfers between devices with their start and end apart: 4, of which 4 were waited for; matrix products, arithmetic and copies ran while one was open for 10% of the time, Pallas kernels for 0%

profile of v1, /device:TPU:6, one launch (start us, length us, event | category | flops | bytes accessed | tf_op | source)
XLA Modules:
  0.0 220.2 jit_solution(16439401994557042852)
XLA Ops:
  0.6 0.0 copy-start
  0.6 0.9 fusion.28
  1.5 0.2 reduce_window_sum.11
  1.7 0.9 select_reduce_fusion
  2.6 0.7 multiply_add_fusion.1
  3.3 1.8 convolution_convert_fusion.4
  5.1 0.0 copy-done.6
  5.1 1.3 convolution_convert_fusion.3
  6.4 0.4 broadcast_in_dim.36
  6.8 2.1 broadcast_in_dim.38
  8.9 2.6 %pad_maximum_fusion.1 = bf16[16,24,8192]{2,1,0:T(8,128)(2,1)S(1)} fusion(bf16[16,24,4096]{2,1,0:T(8,128)(2,1)} %bitcast.59, bf16[16,24,4096]{2,1,0:T(8,128)(2,1)S(1)} %bitcast.58), kind=kLoop, calls=%fused_computation.5 | loop fusion | flops 12582912 | bytes 12582912 | tf_op jit(solution)/shard_map/concatenate | solution.py:46
  11.4 81.2 %all_to_all.10 = bf16[16,24,8192]{2,1,0:T(8,128)(2,1)S(1)} all-to-all(bf16[16,24,8192]{2,1,0:T(8,128)(2,1)S(1)} %pad_maximum_fusion.1), channel_id=1, replica_groups=mesh['section'=4,'chip'=16,'core'=2] {'chip'}, dimensions={0} | all-to-all | bytes 12582912 | tf_op jit(solution)/shard_map/all_to_all | solution.py:22
  92.6 0.0 collective-permute-start
  92.6 10.2 %collective-permute-done = bf16[16,24,8192]{2,1,0:T(8,128)(2,1)S(1)} collective-permute-done((bf16[16,24,8192]{2,1,0:T(8,128)(2,1)S(1)}, bf16[16,24,8192]{2,1,0:T(8,128)(2,1)S(1)}, u32[]{:S(2)}, u32[]{:S(2)}) %collective-permute-start) | collective-permute-done | bytes 6291488 | tf_op jit(solution)/shard_map/ppermute | solution.py:18
  102.8 1.2 pad_maximum_fusion
  104.0 0.0 copy-start.2
  104.0 0.0 copy-done
  104.0 0.0 copy-start.3
  104.0 3.4 %fusion.11 = f32[768,384]{1,0:T(8,128)S(1)} fusion(bf16[768,8192]{1,0:T(8,128)(2,1)S(1)} %bitcast.48, bf16[1,1,4096,384]{3,2,1,0:T(8,128)(2,1)S(1)} %copy-done), kind=kOutput, calls=%fused_computation.20 | convolution fusion | flops 2415919104 | bytes 10616832 | tf_op jit(solution)/shard_map/dot_general | solution.py:12
  107.4 0.8 copy-done.3
  108.2 3.4 %fusion.13 = f32[768,384]{1,0:T(8,128)S(1)} fusion(bf16[768,8192]{1,0:T(8,128)(2,1)S(1)} %bitcast.49, bf16[1,1,4096,384]{3,2,1,0:T(8,128)(2,1)S(1)} %copy-done.3), kind=kOutput, calls=%fused_computation.22 | convolution fusion | flops 2415919104 | bytes 10616832 | tf_op jit(solution)/shard_map/dot_general | solution.py:12
  111.7 3.8 %multiply_convert_fusion.1 = (bf16[768,384]{1,0:T(8,128)(2,1)S(1)}, bf16[768,384]{1,0:T(8,128)(2,1)S(1)}) fusion(f32[768,384]{1,0:T(8,128)S(1)} %fusion.11, f32[768,384]{1,0:T(8,128)S(1)} %fusion.13, bf16[1,1,384,4096]{3,2,1,0:T(8,128)(2,1)S(1)} %copy-done.8, bf16[768,8192]{1,0:T(8,128)(2,1)S(1)} %bitcast.50), kind=kOutput, calls=%fused_computation.33 | convolution fusion | flops 2419752960 | bytes 12976128 | tf_op jit(solution)/shard_map/dot_general | solution.py:12
  115.5 0.0 copy-start.7
  115.5 0.0 copy-start.4
  115.5 3.5 %fusion.15 = f32[768,4096]{1,0:T(8,128)S(1)} fusion(bf16[768,384]{1,0:T(8,128)(2,1)S(1)} %get-tuple-element.5, bf16[1,1,4096,384]{3,2,1,0:T(8,128)(2,1)S(1)} %copy-done), kind=kOutput, calls=%fused_computation.24 | convolution fusion | flops 2415919104 | bytes 16318464 | tf_op jit(solution)/shard_map/dot_general | solution.py:12
  119.0 0.0 copy-done.7
  119.0 0.0 copy-done.4
  119.0 6.3 %convolution_add_fusion = f32[768,4096]{1,0:T(8,128)} fusion(f32[768,4096]{1,0:T(8,128)S(1)} %fusion.15, bf16[768,384]{1,0:T(8,128)(2,1)S(1)} %get-tuple-element.4, bf16[1,1,4096,384]{3,2,1,0:T(8,128)(2,1)S(1)} %copy-done.3), kind=kOutput, calls=%fused_computation.1 | convolution fusion | flops 2419064832 | bytes 28901376 | tf_op jit(solution)/shard_map/dot_general | solution.py:12
  125.3 3.2 %slice.39 = bf16[384,4096]{1,0:T(8,128)(2,1)S(1)} slice(f32[768,4096]{1,0:T(8,128)} %convolution_add_fusion), slice={[384:768], [0:4096]} | slice | bytes 6291456 | tf_op jit(solution)/shard_map/slice | solution.py:63
  128.6 0.4 collective-permute-start.1
  129.0 5.5 %collective-permute-done.1 = bf16[384,4096]{1,0:T(8,128)(2,1)S(1)} collective-permute-done((bf16[384,4096]{1,0:T(8,128)(2,1)S(1)}, bf16[384,4096]{1,0:T(8,128)(2,1)S(1)}, u32[]{:S(2)}, u32[]{:S(2)}) %collective-permute-start.1) | collective-permute-done | bytes 3145760 | tf_op jit(solution)/shard_map/ppermute | solution.py:18
  134.5 5.4 %fusion = bf16[384,4096]{1,0:T(8,128)(2,1)} fusion(f32[768,4096]{1,0:T(8,128)} %convolution_add_fusion, bf16[384,4096]{1,0:T(8,128)(2,1)S(1)} %collective-permute-done.1), kind=kLoop, calls=%fused_computation.4 | loop fusion | flops 4718592 | bytes 12582912 | tf_op jit(solution)/shard_map/convert_element_type | solution.py:64
  139.9 3.7 %all-to-all-start.1 = ((bf16[16,24,4096]{2,1,0:T(8,128)(2,1)}), bf16[16,24,4096]{2,1,0:T(8,128)(2,1)S(1)}, u32[]{:S(2)}, u32[]{:S(2)}) async-start(bf16[16,24,4096]{2,1,0:T(8,128)(2,1)} %bitcast.57), calls=%async_computation.1 | async-start | bytes 6291456 | tf_op jit(solution)/shard_map/all_to_all | solution.py:22
  143.7 0.1 compare_convert_fusion
  143.8 8.0 %fusion.4 = bf16[1,1,4096,384]{3,2,1,0:T(8,128)(2,1)} fusion(bf16[768,384]{1,0:T(8,128)(2,1)} %copy-done.7, bf16[768,8192]{1,0:T(8,128)(2,1)} %bitcast.51), kind=kOutput, calls=%fused_computation.12 | convolution fusion | flops 2417491968 | bytes 10027008 | tf_op jit(solution)/shard_map/dot_general | solution.py:12
  151.8 40.9 %all-to-all-done.1 = bf16[16,24,4096]{2,1,0:T(8,128)(2,1)S(1)} async-done(((bf16[16,24,4096]{2,1,0:T(8,128)(2,1)}), bf16[16,24,4096]{2,1,0:T(8,128)(2,1)S(1)}, u32[]{:S(2)}, u32[]{:S(2)}) %all-to-all-start.1) | async-done | bytes 3145760 | tf_op jit(solution)/shard_map/all_to_all | solution.py:22
  192.7 0.0 slice-start
  192.7 0.7 convolution_convert_fusion.5
  193.5 0.0 slice-start.1
  193.5 0.0 slice-start.2
  193.5 0.9 collective-permute-start.2
  194.4 8.7 %fusion.5 = bf16[1,1,4096,384]{3,2,1,0:T(8,128)(2,1)} fusion(bf16[768,384]{1,0:T(8,128)(2,1)S(1)} %copy-done.5, bf16[768,8192]{1,0:T(8,128)(2,1)} %bitcast.52), kind=kOutput, calls=%fused_computation.13 | convolution fusion | flops 2417491968 | bytes 10027008 | tf_op jit(solution)/shard_map/dot_general | solution.py:12
  203.1 0.0 slice-done
  203.1 0.0 slice-done.2
  203.2 0.0 copy-start.1
  203.2 4.2 %fusion.6 = bf16[1,1,384,4096]{3,2,1,0:T(8,128)(2,1)} fusion(bf16[768,8192]{1,0:T(8,128)(2,1)S(1)} %bitcast.55, f32[768,384]{1,0:T(8,128)S(1)} %copy-done.12, f32[768,384]{1,0:T(8,128)S(1)} %copy-done.10), kind=kOutput, calls=%fused_computation.14 | convolution fusion | flops 2419261440 | bytes 11796480 | tf_op jit(solution)/shard_map/dot_general | solution.py:12
  207.4 11.8 %collective-permute-done.2 = bf16[128,4096]{1,0:T(8,128)(2,1)S(1)} collective-permute-done((bf16[128,4096]{1,0:T(8,128)(2,1)S(1)}, bf16[128,4096]{1,0:T(8,128)(2,1)S(1)}, u32[]{:S(2)}, u32[]{:S(2)}) %collective-permute-start.2) | collective-permute-done | bytes 1048608 | tf_op jit(solution)/shard_map/ppermute | solution.py:73
  219.2 1.0 copy.12
  (19 shorter events, 0.1 us)
Async XLA Ops:
  0.6 103.3 %copy-start = (bf16[1,1,4096,384]{3,2,1,0:T(8,128)(2,1)S(1)}, bf16[1,1,4096,384]{3,2,1,0:T(8,128)(2,1)}, u32[]{:S(2)}) copy-start(bf16[1,1,4096,384]{3,2,1,0:T(8,128)(2,1)} %param.11) | copy-start | bytes 9437188
  1.7 3.4 %copy-start.6 = (bf16[1,128,4096]{2,1,0:T(8,128)(2,1)S(1)}, bf16[1,128,4096]{2,1,0:T(8,128)(2,1)}, u32[]{:S(2)}) copy-start(bf16[1,128,4096]{2,1,0:T(8,128)(2,1)} %param.8) | copy-start | bytes 3145732
  92.6 10.2 %collective-permute-start = (bf16[16,24,8192]{2,1,0:T(8,128)(2,1)S(1)}, bf16[16,24,8192]{2,1,0:T(8,128)(2,1)S(1)}, u32[]{:S(2)}, u32[]{:S(2)}) collective-permute-start(bf16[16,24,8192]{2,1,0:T(8,128)(2,1)S(1)} %all_to_all.10), channel_id=1, source_target_pairs={{0,1},{1,0},{2,3},{3,2},{4,5},{5,4},{6,7},{7,6},{8,9},{9,8},{10,11... | collective-permute-start | bytes 18874376 | tf_op jit(solution)/shard_map/ppermute | solution.py:18
  104.0 7.7 %copy-start.2 = (bf16[32,24,8192]{2,1,0:T(8,128)(2,1)}, bf16[32,24,8192]{2,1,0:T(8,128)(2,1)S(1)}, u32[]{:S(2)}) copy-start(bf16[32,24,8192]{2,1,0:T(8,128)(2,1)S(1)} %pad_maximum_fusion) | copy-start | bytes 37748740
  104.0 4.3 %copy-start.3 = (bf16[1,1,4096,384]{3,2,1,0:T(8,128)(2,1)S(1)}, bf16[1,1,4096,384]{3,2,1,0:T(8,128)(2,1)}, u32[]{:S(2)}) copy-start(bf16[1,1,4096,384]{3,2,1,0:T(8,128)(2,1)} %param.12) | copy-start | bytes 9437188
  108.2 3.4 %copy-start.9 = (f32[768,384]{1,0:T(8,128)}, f32[768,384]{1,0:T(8,128)S(1)}, u32[]{:S(2)}) copy-start(f32[768,384]{1,0:T(8,128)S(1)} %fusion.11) | copy-start | bytes 3538948
  108.2 3.5 %copy-start.8 = (bf16[1,1,384,4096]{3,2,1,0:T(8,128)(2,1)S(1)}, bf16[1,1,384,4096]{3,2,1,0:T(8,128)(2,1)}, u32[]{:S(2)}) copy-start(bf16[1,1,384,4096]{3,2,1,0:T(8,128)(2,1)} %param.13) | copy-start | bytes 9437188
  111.7 3.8 %copy-start.11 = (f32[768,384]{1,0:T(8,128)}, f32[768,384]{1,0:T(8,128)S(1)}, u32[]{:S(2)}) copy-start(f32[768,384]{1,0:T(8,128)S(1)} %fusion.13) | copy-start | bytes 3538948
  115.5 3.5 %copy-start.7 = (bf16[768,384]{1,0:T(8,128)(2,1)}, bf16[768,384]{1,0:T(8,128)(2,1)S(1)}, u32[]{:S(2)}) copy-start(bf16[768,384]{1,0:T(8,128)(2,1)S(1)} %get-tuple-element.5) | copy-start | bytes 1769476
  115.5 3.5 %copy-start.4 = (bf16[768,384]{1,0:T(8,128)(2,1)}, bf16[768,384]{1,0:T(8,128)(2,1)S(1)}, u32[]{:S(2)}) copy-start(bf16[768,384]{1,0:T(8,128)(2,1)S(1)} %get-tuple-element.4) | copy-start | bytes 1769476
  128.6 6.0 %collective-permute-start.1 = (bf16[384,4096]{1,0:T(8,128)(2,1)S(1)}, bf16[384,4096]{1,0:T(8,128)(2,1)S(1)}, u32[]{:S(2)}, u32[]{:S(2)}) collective-permute-start(bf16[384,4096]{1,0:T(8,128)(2,1)S(1)} %slice.39), channel_id=1, source_target_pairs={{0,1},{1,0},{2,3},{3,2},{4,5},{5,4},{6,7},{7,6},{8,9},{9,8},{10,11... | collective-permute-start | bytes 9437192 | tf_op jit(solution)/shard_map/ppermute | solution.py:18
  139.9 52.8 %all-to-all-start.1 = ((bf16[16,24,4096]{2,1,0:T(8,128)(2,1)}), bf16[16,24,4096]{2,1,0:T(8,128)(2,1)S(1)}, u32[]{:S(2)}, u32[]{:S(2)}) async-start(bf16[16,24,4096]{2,1,0:T(8,128)(2,1)} %bitcast.57), calls=%async_computation.1 | async-start | bytes 6291456 | tf_op jit(solution)/shard_map/all_to_all | solution.py:22
  192.7 1.7 copy-start.5
  192.7 10.4 %slice-start = ((s8[12582912]{0:T(1024)(128)(4,1)}), s8[4194304]{0:T(1024)(128)(4,1)S(1)}, s32[]{:S(2)}) async-start(s8[12582912]{0:T(1024)(128)(4,1)} %bitcast.53), calls=%async_computation.2 | async-start | bytes 8388608
  193.5 9.6 %slice-start.1 = ((s8[12582912]{0:T(1024)(128)(4,1)}), s8[4194304]{0:T(1024)(128)(4,1)S(1)}, s32[]{:S(2)}) async-start(s8[12582912]{0:T(1024)(128)(4,1)} %bitcast.53), calls=%async_computation.3 | async-start | bytes 8388608
  193.5 9.6 %slice-start.2 = ((s8[12582912]{0:T(1024)(128)(4,1)}), s8[4194304]{0:T(1024)(128)(4,1)S(1)}, s32[]{:S(2)}) async-start(s8[12582912]{0:T(1024)(128)(4,1)} %bitcast.53), calls=%async_computation.4 | async-start | bytes 8388608
  193.5 9.6 %copy-start.10 = (f32[768,384]{1,0:T(8,128)S(1)}, f32[768,384]{1,0:T(8,128)}, u32[]{:S(2)}) copy-start(f32[768,384]{1,0:T(8,128)} %copy-done.9) | copy-start | bytes 3538948
  193.5 9.6 %copy-start.12 = (f32[768,384]{1,0:T(8,128)S(1)}, f32[768,384]{1,0:T(8,128)}, u32[]{:S(2)}) copy-start(f32[768,384]{1,0:T(8,128)} %copy-done.11) | copy-start | bytes 3538948
  193.5 25.7 %collective-permute-start.2 = (bf16[128,4096]{1,0:T(8,128)(2,1)S(1)}, bf16[128,4096]{1,0:T(8,128)(2,1)S(1)}, u32[]{:S(2)}, u32[]{:S(2)}) collective-permute-start(bf16[128,4096]{1,0:T(8,128)(2,1)S(1)} %convolution_convert_fusion.5), channel_id=1, source_target_pairs={{0,96},{32,0},{64,32},{96,64},{1,97},{33,1},{65,33},{97,65},{2,98}... | collective-permute-start | bytes 3145736 | tf_op jit(solution)/shard_map/ppermute | solution.py:73
  203.2 17.0 %copy-start.1 = (bf16[1,1,4096,384]{3,2,1,0:T(8,128)(2,1)S(1)}, bf16[1,1,4096,384]{3,2,1,0:T(8,128)(2,1)}, u32[]{:S(2)}) copy-start(bf16[1,1,4096,384]{3,2,1,0:T(8,128)(2,1)} %param.11) | copy-start | bytes 9437188

commit v2 on v1

v2 whole, which is shorter than its diff:
```python
import functools

import jax
import jax.numpy as jnp
from jax import lax
from jax.experimental import pallas as pl
from jax.experimental.pallas import tpu as pltpu
from jax.sharding import Mesh, PartitionSpec as P

SPLIT = 4
CORES = 2
HALVES = SPLIT // CORES
MIB = 1 << 20
LIMIT = 56 * MIB
NEXT_LAST = (((1,), (1,)), ((), ()))
FIRST_FIRST = (((0,), (0,)), ((), ()))


def dot(left, right, dims=(((1,), (0,)), ((), ()))):
    return lax.dot_general(left, right, dims, preferred_element_type=jnp.float32)


def swap_cores(value):
    return lax.ppermute(value, "core", [(0, 1), (1, 0)])


def over_chips(value):
    return lax.all_to_all(value, "chip", split_axis=0, concat_axis=0, tiled=True)


def cost(flops, moved):
    return pl.CostEstimate(flops=flops, bytes_accessed=moved, transcendentals=0)


def places(ids, rank, chunks, experts, slot_dim, shape):
    found = []
    at = 0
    for depth in chunks:
        slot = lax.broadcasted_iota(jnp.int32, shape(experts * HALVES * depth), slot_dim)
        inside = (rank >= at) & (rank < at + depth)
        first = ids * (HALVES * depth) + rank - at
        hit = (slot == first) | (slot == first + depth)
        found.append((hit & inside).astype(jnp.float32).astype(jnp.bfloat16))
        at += depth
    return found


def deal_kernel(experts, chunks, blocks, row_ids, col_ids, gates, stash, out_grad, *refs):
    number = len(chunks)
    dealt, place_back, place = refs[:number], refs[number : 2 * number], refs[2 * number :]
    step = pl.program_id(0)
    tokens = col_ids.shape[0]

    @pl.when(step == 0)
    def _():
        first = lax.broadcasted_iota(jnp.int32, (tokens, tokens), 0)
        second = lax.broadcasted_iota(jnp.int32, (tokens, tokens), 1)
        ids = row_ids[...]
        hot = (lax.broadcasted_iota(jnp.int32, (experts, tokens), 0) == ids).astype(jnp.float32)
        before = dot(hot.astype(jnp.bfloat16), (first < second).astype(jnp.bfloat16))
        rank = jnp.sum(before * hot, axis=0, keepdims=True).astype(jnp.int32)
        found = places(ids, rank, chunks, experts, 0, lambda slots: (slots, tokens))
        for ref, value in zip(place, found):
            ref[...] = value
        ids = col_ids[...]
        hot = (lax.broadcasted_iota(jnp.int32, (tokens, experts), 1) == ids).astype(jnp.float32)
        before = dot((second < first).astype(jnp.bfloat16), hot.astype(jnp.bfloat16))
        rank = jnp.sum(before * hot, axis=1, keepdims=True).astype(jnp.int32)
        found = places(ids, rank, chunks, experts, 1, lambda slots: (tokens, slots))
        for ref, value in zip(place_back, found):
            ref[...] = value

    @pl.when(step < blocks)
    def _():
        for ref, at in zip(dealt, place):
            ref[...] = dot(at[...], stash[...]).astype(jnp.bfloat16)

    @pl.when(step >= blocks)
    def _():
        scaled = (gates[...] * out_grad[...].astype(jnp.float32)).astype(jnp.bfloat16)
        for ref, at in zip(dealt, place):
            ref[...] = dot(at[...], scaled).astype(jnp.bfloat16)


def deal(ids, gates, stash, out_grad, experts, chunks):
    tokens, width = stash.shape
    slots = [experts * HALVES * depth for depth in chunks]
    blocks = 4
    span = width // blocks
    outs = pl.pallas_call(
        functools.partial(deal_kernel, experts, chunks, blocks),
        grid=(2 * blocks,),
        in_specs=[
            pl.BlockSpec((1, tokens), lambda i: (0, 0)),
            pl.BlockSpec((tokens, 1), lambda i: (0, 0)),
            pl.BlockSpec((tokens, 1), lambda i: (0, 0)),
            pl.BlockSpec((tokens, span), lambda i: (0, jnp.minimum(i, blocks - 1))),
            pl.BlockSpec((tokens, span), lambda i: (0, jnp.maximum(i - blocks, 0))),
        ],
        out_specs=[pl.BlockSpec((count, span), lambda i: (0, i)) for count in slots]
        + [pl.BlockSpec((tokens, count), lambda i: (0, 0)) for count in slots],
        out_shape=[jax.ShapeDtypeStruct((count, 2 * width), jnp.bfloat16) for count in slots]
        + [jax.ShapeDtypeStruct((tokens, count), jnp.bfloat16) for count in slots],
        scratch_shapes=[pltpu.VMEM((count, tokens), jnp.bfloat16) for count in slots],
        compiler_params=pltpu.CompilerParams(vmem_limit_bytes=LIMIT),
        cost_estimate=cost(4 * sum(slots) * tokens * width, 6 * sum(slots) * width),
        name="deal_rows",
    )(ids.reshape(1, tokens), ids, gates, stash, out_grad)
    return outs[: len(chunks)], outs[len(chunks) :]


def middle_kernel(steps, rows_ref, go, uo, do, gs, us, ds, back, hidden, deltas, *scratch):
    held, joined, down, pre, tail, sems = scratch
    rows, width = back.shape
    units = go.shape[1]
    span = width // steps

    def copies(k):
        at = pl.ds(pl.multiple_of(k * span, span), span)
        late = pl.ds(pl.multiple_of(width + k * span, span), span)
        pairs = [
            (rows_ref.at[:, at], held.at[:, at]),
            (rows_ref.at[:, late], held.at[:, late]),
            (do.at[:, at], down.at[pl.ds(0, units), at]),
            (ds.at[:, at], down.at[pl.ds(units, units), at]),
        ]
        for i, weight in enumerate((go, uo, gs, us)):
            pairs.append((weight.at[at, :], joined.at[at, pl.ds(i * units, units)]))
        return [
            pltpu.make_async_copy(src, dst, sems.at[i, k]) for i, (src, dst) in enumerate(pairs)
        ]

    @pl.loop(0, steps)
    def _(k):
        for copy in copies(k):
            copy.start()

    pre[...] = jnp.zeros_like(pre)
    tail[...] = jnp.zeros_like(tail)

    @pl.loop(0, steps)
    def _(k):
        for copy in copies(k):
            copy.wait()
        at = pl.ds(pl.multiple_of(k * span, span), span)
        late = pl.ds(pl.multiple_of(width + k * span, span), span)
        pre[...] += dot(held[:, at], joined[at, :])
        tail[...] += dot(held[:, late], down[:, at], NEXT_LAST)

    @pl.loop(0, rows // 16)
    def _(r):
        at = pl.ds(pl.multiple_of(r * 16, 16), 16)
        for core in range(CORES):
            gate = slice(2 * core * units, (2 * core + 1) * units)
            up = slice((2 * core + 1) * units, (2 * core + 2) * units)
            own = slice(core * units, (core + 1) * units)
            gate_pre, up_pre, grad = pre[at, gate], pre[at, up], tail[at, own]
            sigmoid_a = jax.nn.sigmoid(gate_pre)
            silu_a = gate_pre * sigmoid_a
            hidden[at, own] = (silu_a * up_pre).astype(jnp.bfloat16)
            deltas[at, gate] = (
                grad * up_pre * sigmoid_a * (1.0 + gate_pre * (1.0 - sigmoid_a))
            ).astype(jnp.bfloat16)
            deltas[at, up] = (grad * silu_a).astype(jnp.bfloat16)

    @pl.loop(0, steps)
    def _(k):
        at = pl.ds(pl.multiple_of(k * span, span), span)
        back[:, at] = dot(deltas[...], joined[at, :], NEXT_LAST).astype(jnp.bfloat16)


def middle(rows, own, sibling):
    count, width = rows.shape[0], rows.shape[1] // 2
    units = own[0].shape[1]
    steps = 4
    anywhere = pl.BlockSpec(memory_space=pl.ANY)
    whole = pl.BlockSpec(memory_space=pltpu.VMEM)
    return pl.pallas_call(
        functools.partial(middle_kernel, steps),
        in_specs=[anywhere] * 7,
        out_specs=[whole] * 3,
        out_shape=[
            jax.ShapeDtypeStruct((count, width), jnp.bfloat16),
            jax.ShapeDtypeStruct((count, CORES * units), jnp.bfloat16),
            jax.ShapeDtypeStruct((count, 2 * CORES * units), jnp.bfloat16),
        ],
        scratch_shapes=[
            pltpu.VMEM((count, 2 * width), jnp.bfloat16),
            pltpu.VMEM((width, 2 * CORES * units), jnp.bfloat16),
            pltpu.VMEM((CORES * units, width), jnp.bfloat16),
            pltpu.VMEM((count, 2 * CORES * units), jnp.float32),
            pltpu.VMEM((count, CORES * units), jnp.float32),
            pltpu.SemaphoreType.DMA((8, steps)),
        ],
        compiler_params=pltpu.CompilerParams(vmem_limit_bytes=LIMIT),
        cost_estimate=cost(10 * count * width * CORES * units, 30 * MIB),
        name="middle",
    )(rows, *own, *sibling)


def grads_kernel(number, added, *refs):
    tokens, grads, hidden, deltas = (refs[i * number : (i + 1) * number] for i in range(4))
    gate, up, down = refs[-3:]
    units = gate.shape[1]
    both = sum(dot(t[...], d[...], FIRST_FIRST) for t, d in zip(tokens, deltas))
    low = sum(dot(h[...], g[...], FIRST_FIRST) for h, g in zip(hidden, grads))
    parts = [both[:, :units], both[:, units:], low]
    if added:
        received = refs[4 * number : 4 * number + 3]
        parts = [part + ref[...].astype(jnp.float32) for part, ref in zip(parts, received)]
    for ref, part in zip((gate, up, down), parts):
        ref[...] = part.astype(jnp.bfloat16)


def weight_grads(rows, hidden, deltas, core, received=()):
    counts = [part.shape[0] for part in rows]
    width = rows[0].shape[1] // 2
    units = hidden[0].shape[1] // CORES
    steps = 8
    span = width // steps
    tall = pl.BlockSpec((span, units), lambda i: (i, 0))
    wide = pl.BlockSpec((units, span), lambda i: (0, i))
    return pl.pallas_call(
        functools.partial(grads_kernel, len(rows), len(received) > 0),
        grid=(steps,),
        in_specs=[pl.BlockSpec((count, span), lambda i: (0, i)) for count in counts]
        + [pl.BlockSpec((count, span), lambda i: (0, i + steps)) for count in counts]
        + [pl.BlockSpec((count, units), lambda i: (0, core)) for count in counts]
        + [pl.BlockSpec((count, 2 * units), lambda i: (0, core)) for count in counts]
        + [tall, tall, wide][: len(received)],
        out_specs=[tall, tall, wide],
        out_shape=[
            jax.ShapeDtypeStruct((width, units), jnp.bfloat16),
            jax.ShapeDtypeStruct((width, units), jnp.bfloat16),
            jax.ShapeDtypeStruct((units, width), jnp.bfloat16),
        ],
        compiler_params=pltpu.CompilerParams(vmem_limit_bytes=LIMIT),
        cost_estimate=cost(6 * sum(counts) * width * units, 16 * MIB),
        name="own_grads" if received else "sibling_grads",
    )(*rows, *rows, *hidden, *deltas, *received)


def body(stash, out_grad, expert_ids, gate_probs, w_gate, w_up, w_down):
    chips = lax.axis_size("chip")
    sections = lax.axis_size("section")
    tokens = stash.shape[1]
    experts = chips * CORES // SPLIT
    capacity = tokens * 3 // (2 * experts)
    chunks = (2 * capacity // 3, capacity // 3)
    own = (w_gate[0, 0], w_up[0, 0], w_down[0, 0])
    sibling = tuple(swap_cores(weight) for weight in own)
    dealt, place_back = deal(
        expert_ids[0], gate_probs[0], stash[0], out_grad[0], experts, chunks
    )
    dealt, sibling = lax.optimization_barrier((dealt, sibling))
    rows = [over_chips(part) for part in dealt]
    hidden, deltas, returned = [], [], []
    back = None
    for part in rows:
        if back is not None:
            part, _ = lax.optimization_barrier((part, back))
        back, part_hidden, part_deltas = middle(part, own, sibling)
        returned.append(over_chips(back))
        hidden.append(part_hidden)
        deltas.append(part_deltas)
    input_grad = sum(dot(at, part) for at, part in zip(place_back, returned)).astype(jnp.bfloat16)
    prev_grad = lax.ppermute(
        input_grad, "section", [(i, (i - 1) % sections) for i in range(sections)]
    )
    theirs = weight_grads(rows, hidden, deltas, 1)
    received = tuple(swap_cores(part) for part in theirs)
    grads = weight_grads(rows, hidden, deltas, 0, received)
    return (prev_grad[None],) + tuple(grad[None, None] for grad in grads)


def solution(mesh):
    sections, devices = mesh.devices.shape
    fine = Mesh(mesh.devices.reshape(sections, devices // CORES, CORES), ("section", "chip", "core"))
    spec = P("section", ("chip", "core"))
    return jax.shard_map(
        body, mesh=fine, in_specs=(spec,) * 7, out_specs=(spec,) * 4, check_vma=False
    )
```

time: 221 us -> 206 us (0.932)
  Pallas kernels: 0 us -> 62.3 us
  matrix products: 45.1 us -> 2.46 us
  blocking collectives: 81.2 us -> 59.3 us
  other arithmetic: 11.9 us -> 0 us
  starting transfers between devices: 5.08 us -> 14.1 us
  waiting for transfers between devices: 68.4 us -> 62.1 us
  local copies, waits for them, and re-layouts: 7.53 us -> 3.77 us
    pallas_call x0 -> x5, Pallas kernels: none -> 62.3 us  [the longest x2 29.4 us: middle(): pl.pallas_call(functools.partial(middle_kernel, steps), in_specs=[anywher...]
    dot_general x11 -> x2, matrix products: 45.1 us -> 2.46 us  [dot(): lax.dot_general(left, right, dims, preferred_element_type=jnp.float32)]
    all_to_all x1, blocking collectives: 81.2 us -> 59.3 us  [over_chips(): lax.all_to_all(value, 'chip', split_axis=0, concat_axis=0, tiled=True)]
    ppermute x1, waiting for transfers between devices: 11.8 us -> 24.3 us  [body(): lax.ppermute(input_grad, 'section', [(i, (i - 1) % sections) for i in ran...]
    ppermute x2 -> x6, waiting for transfers between devices: 15.7 us -> 3.35 us  [swap_cores(): return lax.ppermute(value, 'core', [(0, 1), (1, 0)])]
    all_to_all x1 -> x3, starting transfers between devices: 3.74 us -> 12 us  [over_chips(): lax.all_to_all(value, 'chip', split_axis=0, concat_axis=0, tiled=True)]
    all_to_all x1 -> x3, waiting for transfers between devices: 40.9 us -> 34.5 us  [over_chips(): lax.all_to_all(value, 'chip', split_axis=0, concat_axis=0, tiled=True)]
    convert_element_type x3 -> x0, other arithmetic: 6.39 us -> none  [the longest x1 5.41 us: body(): back = (row_grads[:rows] + theirs.astype(jnp.float32)).astype(jnp.bfloat16)]
  transfers between devices with their start and end apart: 4 -> 10, of which waited for: 4 -> 5; matrix products, arithmetic and copies ran while one was open for 10% -> 3% of each run, Pallas kernels for 0% -> 24%
where the time goes in v2:
time: 206 us; the launch traced here: 205 us
  Pallas kernels  62.3 us (30%)
  waiting for transfers between devices  62.1 us (30%)
  blocking collectives  59.3 us (29%)
  starting transfers between devices  14.1 us (7%)
  local copies, waits for them, and re-layouts  3.77 us (2%)
  matrix products  2.46 us (1%)
    all_to_all x1, blocking collectives, over_chips(): lax.all_to_all(value, 'chip', split_axis=0, concat_axis=0, tiled=True)  59.3 us
    all_to_all x3, waiting for transfers between devices, over_chips(): lax.all_to_all(value, 'chip', split_axis=0, concat_axis=0, tiled=True)  34.5 us
    pallas_call x2, Pallas kernels, middle(): pl.pallas_call(functools.partial(middle_kernel, steps), in_specs=[anywher...  29.4 us
    pallas_call x2, Pallas kernels, weight_grads(): pl.pallas_call(functools.partial(grads_kernel, len(rows), len(received) >...  24.6 us
    ppermute x1, waiting for transfers between devices, body(): lax.ppermute(input_grad, 'section', [(i, (i - 1) % sections) for i in ran...  24.3 us
    all_to_all x3, starting transfers between devices, over_chips(): lax.all_to_all(value, 'chip', split_axis=0, concat_axis=0, tiled=True)  12 us
    pallas_call x1, Pallas kernels, deal(): pl.pallas_call(functools.partial(deal_kernel, experts, chunks, blocks), g...  8.24 us
  transfers between devices with their start and end apart: 10, of which 5 were waited for; matrix products, arithmetic and copies ran while one was open for 3% of the time, Pallas kernels for 24%

profile of v2, /device:TPU:6, one launch (start us, length us, event | category | flops | bytes accessed | tf_op | source)
XLA Modules:
  0.0 204.9 jit_solution(16663514016855778596)
XLA Ops:
  0.6 0.1 collective-permute-start
  0.7 0.5 collective-permute-start.1
  1.2 0.1 collective-permute-start.2
  1.3 1.4 copy.12.gates
  2.7 1.4 copy.11.col_ids
  4.1 8.2 %deal_rows.1 = (bf16[256,8192]{1,0:T(8,128)(2,1)}, bf16[128,8192]{1,0:T(8,128)(2,1)}, bf16[128,256]{1,0:T(8,128)(2,1)}, bf16[128,128]{1,0:T(8,128)(2,1)}) custom-call(s32[1,128]{1,0:T(1,128)} %bitcast.50, s32[128,1]{1,0:T(8,128)} %copy.11.col_ids, f32[128,1]{1,0:T(8,128)} %copy.12.gates, bf16[128,4096]{1,0:T(8,128)(2,1)} %bitcast.54, bf16[128,4096]{1,0:T(8,128)(2,1)} %bitcast.55), custom_call_target="tpu_custom_call" | custom-call | flops 805306368 | bytes 9437184 | tf_op jit(solution)/shard_map/deal_rows/pallas_call | solution.py:90
  12.3 0.0 collective-permute-done.gs
  12.3 0.0 copy-start.1
  12.4 0.0 collective-permute-done.1.us
  12.4 3.3 %collective-permute-done.2.ds = bf16[384,4096]{1,0:T(8,128)(2,1)} collective-permute-done((bf16[384,4096]{1,0:T(8,128)(2,1)}, bf16[384,4096]{1,0:T(8,128)(2,1)}, u32[]{:S(2)}, u32[]{:S(2)}) %collective-permute-start.2) | collective-permute-done | bytes 3145760 | tf_op jit(solution)/shard_map/ppermute | solution.py:24
  15.7 59.3 %all_to_all.46 = bf16[16,16,8192]{2,1,0:T(8,128)(2,1)} all-to-all(bf16[16,16,8192]{2,1,0:T(8,128)(2,1)} %bitcast.35), channel_id=1, replica_groups=mesh['section'=4,'chip'=16,'core'=2] {'chip'}, dimensions={0} | all-to-all | bytes 8388608 | tf_op jit(solution)/shard_map/all_to_all | solution.py:28
  75.0 0.0 copy-done.1
  75.0 3.7 %all-to-all-start.2 = ((bf16[16,8,8192]{2,1,0:T(8,128)(2,1)}), bf16[16,8,8192]{2,1,0:T(8,128)(2,1)S(1)}, u32[]{:S(2)}, u32[]{:S(2)}) async-start(bf16[16,8,8192]{2,1,0:T(8,128)(2,1)} %bitcast.46), calls=%async_computation.2 | async-start | bytes 4194304 | tf_op jit(solution)/shard_map/all_to_all | solution.py:28
  78.8 15.2 %middle.2 = (bf16[256,4096]{1,0:T(8,128)(2,1)}, bf16[256,768]{1,0:T(8,128)(2,1)}, bf16[256,1536]{1,0:T(8,128)(2,1)}) custom-call(bf16[256,8192]{1,0:T(8,128)(2,1)} %bitcast.25, bf16[4096,384]{1,0:T(8,128)(2,1)} %bitcast.37, bf16[4096,384]{1,0:T(8,128)(2,1)} %bitcast.40, bf16[384,4096]{1,0:T(8,128)(2,1)} %bitcast.43, bf16[4096,384]{1,0:T(8,128)(2,1)} %copy-done.1, ...), custom_call_target="tpu_custom_call" | custom-call | flops 8053063680 | bytes 31457280 | tf_op jit(solution)/shard_map/middle/pallas_call | solution.py:178
  93.9 14.7 %all-to-all-done.2 = bf16[16,8,8192]{2,1,0:T(8,128)(2,1)S(1)} async-done(((bf16[16,8,8192]{2,1,0:T(8,128)(2,1)}), bf16[16,8,8192]{2,1,0:T(8,128)(2,1)S(1)}, u32[]{:S(2)}, u32[]{:S(2)}) %all-to-all-start.2) | async-done | bytes 2097184 | tf_op jit(solution)/shard_map/all_to_all | solution.py:28
  108.6 0.0 copy-start
  108.6 4.4 %all-to-all-start.1 = ((bf16[16,16,4096]{2,1,0:T(8,128)(2,1)}), bf16[16,16,4096]{2,1,0:T(8,128)(2,1)}, u32[]{:S(2)}, u32[]{:S(2)}) async-start(bf16[16,16,4096]{2,1,0:T(8,128)(2,1)} %bitcast.45), calls=%async_computation.1 | async-start | bytes 4194304 | tf_op jit(solution)/shard_map/all_to_all | solution.py:28
  113.0 0.0 copy-done
  113.1 14.2 %middle.3 = (bf16[128,4096]{1,0:T(8,128)(2,1)}, bf16[128,768]{1,0:T(8,128)(2,1)}, bf16[128,1536]{1,0:T(8,128)(2,1)}) custom-call(bf16[128,8192]{1,0:T(8,128)(2,1)} %bitcast.30, bf16[4096,384]{1,0:T(8,128)(2,1)} %bitcast.38, bf16[4096,384]{1,0:T(8,128)(2,1)} %bitcast.41, bf16[384,4096]{1,0:T(8,128)(2,1)} %bitcast.44, bf16[4096,384]{1,0:T(8,128)(2,1)} %copy-done.1, ...), custom_call_target="tpu_custom_call" | custom-call | flops 4026531840 | bytes 31457280 | tf_op jit(solution)/shard_map/middle/pallas_call | solution.py:178
  127.3 0.0 copy-start.2
  127.3 10.9 %sibling_grads.1 = (bf16[4096,384]{1,0:T(8,128)(2,1)}, bf16[4096,384]{1,0:T(8,128)(2,1)}, bf16[384,4096]{1,0:T(8,128)(2,1)}) custom-call(bf16[256,8192]{1,0:T(8,128)(2,1)} %bitcast.26, bf16[128,8192]{1,0:T(8,128)(2,1)} %bitcast.31, bf16[256,8192]{1,0:T(8,128)(2,1)} %bitcast.27, bf16[128,8192]{1,0:T(8,128)(2,1)} %bitcast.32, ...), custom_call_target="tpu_custom_call" | custom-call | flops 3623878656 | bytes 16777216 | tf_op jit(solution)/shard_map/sibling_grads/pallas_call | solution.py:223
  138.2 0.0 collective-permute-start.4
  138.2 0.5 collective-permute-start.5
  138.7 0.1 collective-permute-start.6
  138.8 3.4 %all-to-all-done.1 = bf16[16,16,4096]{2,1,0:T(8,128)(2,1)} async-done(((bf16[16,16,4096]{2,1,0:T(8,128)(2,1)}), bf16[16,16,4096]{2,1,0:T(8,128)(2,1)}, u32[]{:S(2)}, u32[]{:S(2)}) %all-to-all-start.1) | async-done | bytes 2097184 | tf_op jit(solution)/shard_map/all_to_all | solution.py:28
  142.2 0.0 copy-start.3
  142.2 3.8 %all-to-all-start.3 = ((bf16[16,8,4096]{2,1,0:T(8,128)(2,1)}), bf16[16,8,4096]{2,1,0:T(8,128)(2,1)S(1)}, u32[]{:S(2)}, u32[]{:S(2)}) async-start(bf16[16,8,4096]{2,1,0:T(8,128)(2,1)} %bitcast.14), calls=%async_computation.3 | async-start | bytes 2097152 | tf_op jit(solution)/shard_map/all_to_all | solution.py:28
  146.0 0.0 copy-done.2
  146.0 2.0 fusion.2
  148.1 16.4 %all-to-all-done.3 = bf16[16,8,4096]{2,1,0:T(8,128)(2,1)S(1)} async-done(((bf16[16,8,4096]{2,1,0:T(8,128)(2,1)}), bf16[16,8,4096]{2,1,0:T(8,128)(2,1)S(1)}, u32[]{:S(2)}, u32[]{:S(2)}) %all-to-all-start.3) | async-done | bytes 1048608 | tf_op jit(solution)/shard_map/all_to_all | solution.py:28
  164.5 0.0 copy-done.3
  164.5 0.4 fusion
  164.9 0.9 collective-permute-start.3
  165.8 24.3 %collective-permute-done.3 = bf16[128,4096]{1,0:T(8,128)(2,1)S(1)} collective-permute-done((bf16[128,4096]{1,0:T(8,128)(2,1)S(1)}, bf16[128,4096]{1,0:T(8,128)(2,1)S(1)}, u32[]{:S(2)}, u32[]{:S(2)}) %collective-permute-start.3) | collective-permute-done | bytes 1048608 | tf_op jit(solution)/shard_map/ppermute | solution.py:267
  190.1 0.0 collective-permute-done.4.refs_8_
  190.1 0.0 collective-permute-done.5.refs_9_
  190.1 0.0 collective-permute-done.6.refs_10_
  190.1 13.8 %own_grads.1 = (bf16[4096,384]{1,0:T(8,128)(2,1)}, bf16[4096,384]{1,0:T(8,128)(2,1)}, bf16[384,4096]{1,0:T(8,128)(2,1)}) custom-call(bf16[256,8192]{1,0:T(8,128)(2,1)} %bitcast.28, bf16[128,8192]{1,0:T(8,128)(2,1)} %bitcast.33, bf16[256,8192]{1,0:T(8,128)(2,1)} %bitcast.29, bf16[128,8192]{1,0:T(8,128)(2,1)} %bitcast.34, ...), custom_call_target="tpu_custom_call" | custom-call | flops 3623878656 | bytes 16777216 | tf_op jit(solution)/shard_map/own_grads/pallas_call | solution.py:223
  203.9 1.0 copy.14
Async XLA Ops:
  0.6 11.7 %collective-permute-start = (bf16[4096,384]{1,0:T(8,128)(2,1)}, bf16[4096,384]{1,0:T(8,128)(2,1)S(1)}, u32[]{:S(2)}, u32[]{:S(2)}) collective-permute-start(bf16[4096,384]{1,0:T(8,128)(2,1)} %bitcast.36), channel_id=1, source_target_pairs={{0,1},{1,0},{2,3},{3,2},{4,5},{5,4},{6,7},{7,6},{8,9},{9,8},{10,11... | collective-permute-start | bytes 9437192 | tf_op jit(solution)/shard_map/ppermute | solution.py:24
  0.7 11.6 %collective-permute-start.1 = (bf16[4096,384]{1,0:T(8,128)(2,1)}, bf16[4096,384]{1,0:T(8,128)(2,1)}, u32[]{:S(2)}, u32[]{:S(2)}) collective-permute-start(bf16[4096,384]{1,0:T(8,128)(2,1)} %bitcast.39), channel_id=1, source_target_pairs={{0,1},{1,0},{2,3},{3,2},{4,5},{5,4},{6,7},{7,6},{8,9},{9,8},{10,11... | collective-permute-start | bytes 9437192 | tf_op jit(solution)/shard_map/ppermute | solution.py:24
  1.2 14.5 %collective-permute-start.2 = (bf16[384,4096]{1,0:T(8,128)(2,1)}, bf16[384,4096]{1,0:T(8,128)(2,1)}, u32[]{:S(2)}, u32[]{:S(2)}) collective-permute-start(bf16[384,4096]{1,0:T(8,128)(2,1)} %bitcast.42), channel_id=1, source_target_pairs={{0,1},{1,0},{2,3},{3,2},{4,5},{5,4},{6,7},{7,6},{8,9},{9,8},{10,11... | collective-permute-start | bytes 9437192 | tf_op jit(solution)/shard_map/ppermute | solution.py:24
  12.3 62.7 %copy-start.1 = (bf16[4096,384]{1,0:T(8,128)(2,1)}, bf16[4096,384]{1,0:T(8,128)(2,1)S(1)}, u32[]{:S(2)}) copy-start(bf16[4096,384]{1,0:T(8,128)(2,1)S(1)} %collective-permute-done.gs) | copy-start | bytes 9437188
  75.0 33.6 %all-to-all-start.2 = ((bf16[16,8,8192]{2,1,0:T(8,128)(2,1)}), bf16[16,8,8192]{2,1,0:T(8,128)(2,1)S(1)}, u32[]{:S(2)}, u32[]{:S(2)}) async-start(bf16[16,8,8192]{2,1,0:T(8,128)(2,1)} %bitcast.46), calls=%async_computation.2 | async-start | bytes 4194304 | tf_op jit(solution)/shard_map/all_to_all | solution.py:28
  108.6 4.4 %copy-start = (bf16[16,8,8192]{2,1,0:T(8,128)(2,1)}, bf16[16,8,8192]{2,1,0:T(8,128)(2,1)S(1)}, u32[]{:S(2)}) copy-start(bf16[16,8,8192]{2,1,0:T(8,128)(2,1)S(1)} %all-to-all-done.2) | copy-start | bytes 6291460
  108.6 33.6 %all-to-all-start.1 = ((bf16[16,16,4096]{2,1,0:T(8,128)(2,1)}), bf16[16,16,4096]{2,1,0:T(8,128)(2,1)}, u32[]{:S(2)}, u32[]{:S(2)}) async-start(bf16[16,16,4096]{2,1,0:T(8,128)(2,1)} %bitcast.45), calls=%async_computation.1 | async-start | bytes 4194304 | tf_op jit(solution)/shard_map/all_to_all | solution.py:28
  127.3 18.7 %copy-start.2 = (bf16[128,256]{1,0:T(8,128)(2,1)S(1)}, bf16[128,256]{1,0:T(8,128)(2,1)}, u32[]{:S(2)}) copy-start(bf16[128,256]{1,0:T(8,128)(2,1)} %get-tuple-element.26) | copy-start | bytes 196612
  138.2 51.9 %collective-permute-start.4 = (bf16[4096,384]{1,0:T(8,128)(2,1)}, bf16[4096,384]{1,0:T(8,128)(2,1)}, u32[]{:S(2)}, u32[]{:S(2)}) collective-permute-start(bf16[4096,384]{1,0:T(8,128)(2,1)} %get-tuple-element.42), channel_id=1, source_target_pairs={{0,1},{1,0},{2,3},{3,2},{4,5},{5,4},{6,7},{7,6},{8,9},{9,8},{10,11... | collective-permute-start | bytes 9437192 | tf_op jit(solution)/shard_map/ppermute | solution.py:24
  138.2 51.9 %collective-permute-start.5 = (bf16[4096,384]{1,0:T(8,128)(2,1)}, bf16[4096,384]{1,0:T(8,128)(2,1)}, u32[]{:S(2)}, u32[]{:S(2)}) collective-permute-start(bf16[4096,384]{1,0:T(8,128)(2,1)} %get-tuple-element.43), channel_id=1, source_target_pairs={{0,1},{1,0},{2,3},{3,2},{4,5},{5,4},{6,7},{7,6},{8,9},{9,8},{10,11... | collective-permute-start | bytes 9437192 | tf_op jit(solution)/shard_map/ppermute | solution.py:24
  138.7 51.4 %collective-permute-start.6 = (bf16[384,4096]{1,0:T(8,128)(2,1)}, bf16[384,4096]{1,0:T(8,128)(2,1)}, u32[]{:S(2)}, u32[]{:S(2)}) collective-permute-start(bf16[384,4096]{1,0:T(8,128)(2,1)} %get-tuple-element.44), channel_id=1, source_target_pairs={{0,1},{1,0},{2,3},{3,2},{4,5},{5,4},{6,7},{7,6},{8,9},{9,8},{10,11... | collective-permute-start | bytes 9437192 | tf_op jit(solution)/shard_map/ppermute | solution.py:24
  142.2 22.3 %copy-start.3 = (bf16[128,128]{1,0:T(8,128)(2,1)S(1)}, bf16[128,128]{1,0:T(8,128)(2,1)}, u32[]{:S(2)}) copy-start(bf16[128,128]{1,0:T(8,128)(2,1)} %get-tuple-element.34) | copy-start | bytes 98308
  142.2 22.3 %all-to-all-start.3 = ((bf16[16,8,4096]{2,1,0:T(8,128)(2,1)}), bf16[16,8,4096]{2,1,0:T(8,128)(2,1)S(1)}, u32[]{:S(2)}, u32[]{:S(2)}) async-start(bf16[16,8,4096]{2,1,0:T(8,128)(2,1)} %bitcast.14), calls=%async_computation.3 | async-start | bytes 2097152 | tf_op jit(solution)/shard_map/all_to_all | solution.py:28
  164.9 25.2 %collective-permute-start.3 = (bf16[128,4096]{1,0:T(8,128)(2,1)S(1)}, bf16[128,4096]{1,0:T(8,128)(2,1)S(1)}, u32[]{:S(2)}, u32[]{:S(2)}) collective-permute-start(bf16[128,4096]{1,0:T(8,128)(2,1)S(1)} %fusion), channel_id=1, source_target_pairs={{0,96},{32,0},{64,32},{96,64},{1,97},{33,1},{65,33},{97,65},{2,98}... | collective-permute-start | bytes 3145736 | tf_op jit(solution)/shard_map/ppermute | solution.py:267

commit v3 on v2

--- a/solution.py
+++ b/solution.py
@@ -102,22 +102,25 @@
         out_shape=[jax.ShapeDtypeStruct((count, 2 * width), jnp.bfloat16) for count in slots]
         + [jax.ShapeDtypeStruct((tokens, count), jnp.bfloat16) for count in slots],
         scratch_shapes=[pltpu.VMEM((count, tokens), jnp.bfloat16) for count in slots],
-        compiler_params=pltpu.CompilerParams(vmem_limit_bytes=LIMIT),
+        compiler_params=pltpu.CompilerParams(vmem_limit_bytes=16 * MIB),
         cost_estimate=cost(4 * sum(slots) * tokens * width, 6 * sum(slots) * width),
         name="deal_rows",
     )(ids.reshape(1, tokens), ids, gates, stash, out_grad)
     return outs[: len(chunks)], outs[len(chunks) :]
 
 
-def middle_kernel(steps, rows_ref, go, uo, do, gs, us, ds, back, hidden, deltas, *scratch):
-    held, joined, down, pre, tail, sems = scratch
-    rows, width = back.shape
+def middle_kernel(steps, cuts, rows_ref, go, uo, do, gs, us, ds, *refs):
+    backs, refs = refs[: len(cuts)], refs[len(cuts) :]
+    hidden, deltas, held, joined, down, pre, tail, out, sems, out_sems = refs
+    rows, width = out.shape
     units = go.shape[1]
     span = width // steps
 
+    def block(k, base=0):
+        return pl.ds(pl.multiple_of(base + k * span, span), span)
+
     def copies(k):
-        at = pl.ds(pl.multiple_of(k * span, span), span)
-        late = pl.ds(pl.multiple_of(width + k * span, span), span)
+        at, late = block(k), block(k, width)
         pairs = [
             (rows_ref.at[:, at], held.at[:, at]),
             (rows_ref.at[:, late], held.at[:, late]),
@@ -142,8 +145,7 @@
     def _(k):
         for copy in copies(k):
             copy.wait()
-        at = pl.ds(pl.multiple_of(k * span, span), span)
-        late = pl.ds(pl.multiple_of(width + k * span, span), span)
+        at, late = block(k), block(k, width)
         pre[...] += dot(held[:, at], joined[at, :])
         tail[...] += dot(held[:, late], down[:, at], NEXT_LAST)
 
@@ -163,24 +165,40 @@
             ).astype(jnp.bfloat16)
             deltas[at, up] = (grad * silu_a).astype(jnp.bfloat16)
 
-    @pl.loop(0, steps)
-    def _(k):
-        at = pl.ds(pl.multiple_of(k * span, span), span)
-        back[:, at] = dot(deltas[...], joined[at, :], NEXT_LAST).astype(jnp.bfloat16)
-
-
-def middle(rows, own, sibling):
+    def leave(back, k, begin):
+        return pltpu.make_async_copy(out.at[:, block(k)], back.at[:, block(k - begin)], out_sems.at[k])
+
+    begin = 0
+    ranges = []
+    for back, cut in zip(backs, cuts):
+        ranges.append((back, begin, begin + cut // span))
+        begin += cut // span
+    for back, begin, end in ranges:
+
+        @pl.loop(begin, end)
+        def _(k):
+            out[:, block(k)] = dot(deltas[...], joined[block(k), :], NEXT_LAST).astype(jnp.bfloat16)
+            leave(back, k, begin).start()
+
+    for back, begin, end in ranges:
+
+        @pl.loop(begin, end)
+        def _(k):
+            leave(back, k, begin).wait()
+
+
+def middle(rows, own, sibling, cuts):
     count, width = rows.shape[0], rows.shape[1] // 2
     units = own[0].shape[1]
-    steps = 4
+    steps = 8
     anywhere = pl.BlockSpec(memory_space=pl.ANY)
     whole = pl.BlockSpec(memory_space=pltpu.VMEM)
-    return pl.pallas_call(
-        functools.partial(middle_kernel, steps),
+    outs = pl.pallas_call(
+        functools.partial(middle_kernel, steps, cuts),
         in_specs=[anywhere] * 7,
-        out_specs=[whole] * 3,
-        out_shape=[
-            jax.ShapeDtypeStruct((count, width), jnp.bfloat16),
+        out_specs=[anywhere] * len(cuts) + [whole] * 2,
+        out_shape=[jax.ShapeDtypeStruct((count, cut), jnp.bfloat16) for cut in cuts]
+        + [
             jax.ShapeDtypeStruct((count, CORES * units), jnp.bfloat16),
             jax.ShapeDtypeStruct((count, 2 * CORES * units), jnp.bfloat16),
         ],
@@ -190,12 +208,15 @@
             pltpu.VMEM((CORES * units, width), jnp.bfloat16),
             pltpu.VMEM((count, 2 * CORES * units), jnp.float32),
             pltpu.VMEM((count, CORES * units), jnp.float32),
+            pltpu.VMEM((count, width), jnp.bfloat16),
             pltpu.SemaphoreType.DMA((8, steps)),
+            pltpu.SemaphoreType.DMA((steps,)),
         ],
-        compiler_params=pltpu.CompilerParams(vmem_limit_bytes=LIMIT),
+        compiler_params=pltpu.CompilerParams(vmem_limit_bytes=40 * MIB),
         cost_estimate=cost(10 * count * width * CORES * units, 30 * MIB),
         name="middle",
     )(rows, *own, *sibling)
+    return outs[: len(cuts)], outs[-2], outs[-1]
 
 
 def grads_kernel(number, added, *refs):
@@ -246,30 +267,35 @@
     tokens = stash.shape[1]
     experts = chips * CORES // SPLIT
     capacity = tokens * 3 // (2 * experts)
-    chunks = (2 * capacity // 3, capacity // 3)
     own = (w_gate[0, 0], w_up[0, 0], w_down[0, 0])
     sibling = tuple(swap_cores(weight) for weight in own)
-    dealt, place_back = deal(
-        expert_ids[0], gate_probs[0], stash[0], out_grad[0], experts, chunks
+    (dealt,), (place_back,) = deal(
+        expert_ids[0], gate_probs[0], stash[0], out_grad[0], experts, (capacity,)
     )
     dealt, sibling = lax.optimization_barrier((dealt, sibling))
-    rows = [over_chips(part) for part in dealt]
-    hidden, deltas, returned = [], [], []
-    back = None
-    for part in rows:
-        if back is not None:
-            part, _ = lax.optimization_barrier((part, back))
-        back, part_hidden, part_deltas = middle(part, own, sibling)
-        returned.append(over_chips(back))
-        hidden.append(part_hidden)
-        deltas.append(part_deltas)
-    input_grad = sum(dot(at, part) for at, part in zip(place_back, returned)).astype(jnp.bfloat16)
-    prev_grad = lax.ppermute(
-        input_grad, "section", [(i, (i - 1) % sections) for i in range(sections)]
-    )
-    theirs = weight_grads(rows, hidden, deltas, 1)
+    rows = over_chips(dealt)
+    width = stash.shape[2]
+    backs, hidden, deltas = middle(rows, own, sibling, (width * 3 // 4, width // 4))
+    theirs = weight_grads([rows], [hidden], [deltas], 1)
     received = tuple(swap_cores(part) for part in theirs)
-    grads = weight_grads(rows, hidden, deltas, 0, received)
+
+    def shift(returned):
+        input_grad = dot(place_back, returned).astype(jnp.bfloat16)
+        return input_grad, lambda value: lax.ppermute(
+            value, "section", [(i, (i - 1) % sections) for i in range(sections)]
+        )
+
+    first = over_chips(backs[0])
+    last, first = lax.optimization_barrier((backs[1], first))
+    last = over_chips(last)
+    first, move = shift(first)
+    deltas, first = lax.optimization_barrier((deltas, first))
+    first = move(first)
+    grads = weight_grads([rows], [hidden], [deltas], 0, received)
+    last, move = shift(last)
+    last, grads = lax.optimization_barrier((last, tuple(grads)))
+    last = move(last)
+    prev_grad = jnp.concatenate([first, last], axis=1)
     return (prev_grad[None],) + tuple(grad[None, None] for grad in grads)
 
 

time: 206 us -> 196 us (0.951)
  blocking collectives: 59.3 us -> 81.8 us
  waiting for transfers between devices: 62.1 us -> 46 us
  Pallas kernels: 62.3 us -> 47.7 us
  starting transfers between devices: 14.1 us -> 10.1 us
  local copies, waits for them, and re-layouts: 3.77 us -> 6.49 us
    all_to_all x1, blocking collectives: 59.3 us -> 81.8 us  [over_chips(): lax.all_to_all(value, 'chip', split_axis=0, concat_axis=0, tiled=True)]
    ppermute x1 -> x2, waiting for transfers between devices: 24.3 us -> 6.85 us  [shift(): lax.ppermute(value, 'section', [(i, (i - 1) % sections) for i in range(se...]
    pallas_call x2 -> x1, Pallas kernels: 29.4 us -> 19 us  [middle(): pl.pallas_call(functools.partial(middle_kernel, steps, cuts), in_specs=[a...]
    all_to_all x3 -> x2, starting transfers between devices: 12 us -> 7.34 us  [over_chips(): lax.all_to_all(value, 'chip', split_axis=0, concat_axis=0, tiled=True)]
    unnamed x9 -> x18, local copies, waits for them, and re-layouts: 0.99 us -> 4.97 us
    pallas_call x1, Pallas kernels: 8.24 us -> 4.34 us  [deal(): pl.pallas_call(functools.partial(deal_kernel, experts, chunks, blocks), g...]
    all_to_all x3 -> x2, waiting for transfers between devices: 34.5 us -> 33.8 us  [over_chips(): lax.all_to_all(value, 'chip', split_axis=0, concat_axis=0, tiled=True)]
  transfers between devices with their start and end apart: 10 -> 10, of which waited for: 5 -> 5; matrix products, arithmetic and copies ran while one was open for 3% -> 2% of each run, Pallas kernels for 24% -> 15%
where the time goes in v3:
time: 196 us
  blocking collectives  81.8 us (42%)
  Pallas kernels  47.7 us (24%)
  waiting for transfers between devices  46 us (23%)
  starting transfers between devices  10.1 us (5%)
  local copies, waits for them, and re-layouts  6.49 us (3%)
    all_to_all x1, blocking collectives, over_chips(): lax.all_to_all(value, 'chip', split_axis=0, concat_axis=0, tiled=True)  81.8 us
    all_to_all x2, waiting for transfers between devices, over_chips(): lax.all_to_all(value, 'chip', split_axis=0, concat_axis=0, tiled=True)  33.8 us
    pallas_call x2, Pallas kernels, weight_grads(): pl.pallas_call(functools.partial(grads_kernel, len(rows), len(received) >...  24.4 us
    pallas_call x1, Pallas kernels, middle(): pl.pallas_call(functools.partial(middle_kernel, steps, cuts), in_specs=[a...  19 us
    all_to_all x2, starting transfers between devices, over_chips(): lax.all_to_all(value, 'chip', split_axis=0, concat_axis=0, tiled=True)  7.34 us
    ppermute x2, waiting for transfers between devices, shift(): lax.ppermute(value, 'section', [(i, (i - 1) % sections) for i in range(se...  6.85 us
    ppermute x6, waiting for transfers between devices, swap_cores(): return lax.ppermute(value, 'core', [(0, 1), (1, 0)])  5.41 us
    unnamed x18, local copies, waits for them, and re-layouts  4.97 us
  transfers between devices with their start and end apart: 10, of which 5 were waited for; matrix products, arithmetic and copies ran while one was open for 2% of the time, Pallas kernels for 15%

profile of v3, /device:TPU:6, one launch (start us, length us, event | category | flops | bytes accessed | tf_op | source)
XLA Modules:
  0.0 195.7 jit_solution(5281064224419129321)
XLA Ops:
  0.6 0.1 collective-permute-start
  0.7 0.5 collective-permute-start.1
  1.2 0.1 collective-permute-start.2
  1.3 0.8 copy.12.gates
  2.1 0.8 copy.11.col_ids
  2.8 0.0 copy-start.2
  2.8 0.6 copy-done.2
  3.5 0.0 copy-start.6
  3.5 1.2 copy-done.6
  4.7 0.0 copy-start.7
  4.7 1.2 copy-done.7
  5.9 4.3 %deal_rows.1 = (bf16[384,8192]{1,0:T(8,128)(2,1)S(1)}, bf16[128,384]{1,0:T(8,128)(2,1)S(1)}) custom-call(s32[1,128]{1,0:T(1,128)S(1)} %bitcast.25, s32[128,1]{1,0:T(8,128)S(1)} %copy.11.col_ids, f32[128,1]{1,0:T(8,128)S(1)} %copy.12.gates, bf16[128,4096]{1,0:T(8,128)(2,1)S(1)} %bitcast.32, bf16[128,4096]{1,0:T(8,128)(2,1)S(1)} %bitcast.33), custom_call_target="tpu_custom_call" | custom-call | flops 805306368 | bytes 9437184 | tf_op jit(solution)/shard_map/deal_rows/pallas_call | solution.py:90
  10.3 0.0 collective-permute-done.gs
  10.3 0.0 copy-start.8
  10.3 0.9 collective-permute-done.1.us
  11.2 4.5 %collective-permute-done.2.ds = bf16[384,4096]{1,0:T(8,128)(2,1)} collective-permute-done((bf16[384,4096]{1,0:T(8,128)(2,1)}, bf16[384,4096]{1,0:T(8,128)(2,1)}, u32[]{:S(2)}, u32[]{:S(2)}) %collective-permute-start.2) | collective-permute-done | bytes 3145760 | tf_op jit(solution)/shard_map/ppermute | solution.py:24
  15.7 0.0 copy-start.3
  15.7 0.0 copy-start.4
  15.7 0.0 copy-start.5
  15.7 81.8 %all_to_all.35 = bf16[16,24,8192]{2,1,0:T(8,128)(2,1)} all-to-all(bf16[16,24,8192]{2,1,0:T(8,128)(2,1)S(1)} %bitcast.23), channel_id=1, replica_groups=mesh['section'=4,'chip'=16,'core'=2] {'chip'}, dimensions={0} | all-to-all | bytes 12582912 | tf_op jit(solution)/shard_map/all_to_all | solution.py:28
  97.6 0.0 copy-done.8
  97.6 0.0 copy-done.3
  97.6 0.0 copy-done.4
  97.6 0.0 copy-done.5
  97.6 19.0 %middle.1 = (bf16[384,3072]{1,0:T(8,128)(2,1)}, bf16[384,1024]{1,0:T(8,128)(2,1)}, bf16[384,768]{1,0:T(8,128)(2,1)S(1)}, bf16[384,1536]{1,0:T(8,128)(2,1)S(1)}) custom-call(bf16[384,8192]{1,0:T(8,128)(2,1)} %bitcast.34, bf16[4096,384]{1,0:T(8,128)(2,1)S(1)} %bitcast.27, bf16[4096,384]{1,0:T(8,128)(2,1)S(1)} %bitcast.29, bf16[384,4096]{1,0:T(8,128)(2,1)S(1)} %bitcast.31, ...), custom_call_target="tpu_custom_call" | custom-call | flops 12079595520 | bytes 31457280 | tf_op jit(solution)/shard_map/middle/pallas_call | solution.py:196
  116.6 0.0 copy-start
  116.6 1.0 copy-done
  117.6 0.0 copy-start.1
  117.6 0.8 copy-done.1
  118.4 3.7 %all-to-all-start.1 = ((bf16[16,24,3072]{2,1,0:T(8,128)(2,1)}), bf16[16,24,3072]{2,1,0:T(8,128)(2,1)S(1)}, u32[]{:S(2)}, u32[]{:S(2)}) async-start(bf16[16,24,3072]{2,1,0:T(8,128)(2,1)} %bitcast.10), calls=%async_computation.1 | async-start | bytes 4718592 | tf_op jit(solution)/shard_map/all_to_all | solution.py:28
  122.2 10.8 %sibling_grads.1 = (bf16[4096,384]{1,0:T(8,128)(2,1)}, bf16[4096,384]{1,0:T(8,128)(2,1)}, bf16[384,4096]{1,0:T(8,128)(2,1)}) custom-call(bf16[384,8192]{1,0:T(8,128)(2,1)} %bitcast.35, bf16[384,8192]{1,0:T(8,128)(2,1)} %bitcast.36, bf16[384,768]{1,0:T(8,128)(2,1)} %copy-done.1, bf16[384,1536]{1,0:T(8,128)(2,1)} %copy-done), custom_call_target="tpu_custom_call" | custom-call | flops 3623878656 | bytes 16777216 | tf_op jit(solution)/shard_map/sibling_grads/pallas_call | solution.py:244
  132.9 0.0 collective-permute-start.4
  133.0 0.5 collective-permute-start.5
  133.5 0.1 collective-permute-start.6
  133.5 21.8 %all-to-all-done.1 = bf16[16,24,3072]{2,1,0:T(8,128)(2,1)S(1)} async-done(((bf16[16,24,3072]{2,1,0:T(8,128)(2,1)}), bf16[16,24,3072]{2,1,0:T(8,128)(2,1)S(1)}, u32[]{:S(2)}, u32[]{:S(2)}) %all-to-all-start.1) | async-done | bytes 2359328 | tf_op jit(solution)/shard_map/all_to_all | solution.py:28
  155.4 3.6 %all-to-all-start.2 = ((bf16[16,24,1024]{2,1,0:T(8,128)(2,1)}), bf16[16,24,1024]{2,1,0:T(8,128)(2,1)S(1)}, u32[]{:S(2)}, u32[]{:S(2)}) async-start(bf16[16,24,1024]{2,1,0:T(8,128)(2,1)} %bitcast.12), calls=%async_computation.2 | async-start | bytes 1572864 | tf_op jit(solution)/shard_map/all_to_all | solution.py:28
  159.0 1.5 convolution_convert_fusion
  160.5 0.8 collective-permute-start.3
  161.2 12.0 %all-to-all-done.2 = bf16[16,24,1024]{2,1,0:T(8,128)(2,1)S(1)} async-done(((bf16[16,24,1024]{2,1,0:T(8,128)(2,1)}), bf16[16,24,1024]{2,1,0:T(8,128)(2,1)S(1)}, u32[]{:S(2)}, u32[]{:S(2)}) %all-to-all-start.2) | async-done | bytes 786464 | tf_op jit(solution)/shard_map/all_to_all | solution.py:28
  173.2 0.3 convolution_convert_fusion.1
  173.5 0.0 collective-permute-done.4.refs_4_
  173.5 0.0 collective-permute-done.5.refs_5_
  173.5 0.0 collective-permute-done.6.refs_6_
  173.5 13.6 %own_grads.1 = (bf16[4096,384]{1,0:T(8,128)(2,1)}, bf16[4096,384]{1,0:T(8,128)(2,1)}, bf16[384,4096]{1,0:T(8,128)(2,1)}) custom-call(bf16[384,8192]{1,0:T(8,128)(2,1)} %bitcast.37, bf16[384,8192]{1,0:T(8,128)(2,1)} %bitcast.38, bf16[384,768]{1,0:T(8,128)(2,1)} %copy-done.1, bf16[384,1536]{1,0:T(8,128)(2,1)} %copy-done, ...), custom_call_target="tpu_custom_call" | custom-call | flops 3623878656 | bytes 16777216 | tf_op jit(solution)/shard_map/own_grads/pallas_call | solution.py:244
  187.1 0.7 collective-permute-start.7
  187.8 0.0 collective-permute-done.3
  187.8 6.8 %collective-permute-done.7 = bf16[128,1024]{1,0:T(8,128)(2,1)S(1)} collective-permute-done((bf16[128,1024]{1,0:T(8,128)(2,1)S(1)}, bf16[128,1024]{1,0:T(8,128)(2,1)S(1)}, u32[]{:S(2)}, u32[]{:S(2)}) %collective-permute-start.7) | collective-permute-done | bytes 262176 | tf_op jit(solution)/shard_map/ppermute | solution.py:284
  194.7 1.0 maximum_bitcast_fusion
Async XLA Ops:
  0.6 9.7 %collective-permute-start = (bf16[4096,384]{1,0:T(8,128)(2,1)}, bf16[4096,384]{1,0:T(8,128)(2,1)S(1)}, u32[]{:S(2)}, u32[]{:S(2)}) collective-permute-start(bf16[4096,384]{1,0:T(8,128)(2,1)} %bitcast.26), channel_id=1, source_target_pairs={{0,1},{1,0},{2,3},{3,2},{4,5},{5,4},{6,7},{7,6},{8,9},{9,8},{10,11... | collective-permute-start | bytes 9437192 | tf_op jit(solution)/shard_map/ppermute | solution.py:24
  0.7 10.5 %collective-permute-start.1 = (bf16[4096,384]{1,0:T(8,128)(2,1)}, bf16[4096,384]{1,0:T(8,128)(2,1)}, u32[]{:S(2)}, u32[]{:S(2)}) collective-permute-start(bf16[4096,384]{1,0:T(8,128)(2,1)} %bitcast.28), channel_id=1, source_target_pairs={{0,1},{1,0},{2,3},{3,2},{4,5},{5,4},{6,7},{7,6},{8,9},{9,8},{10,11... | collective-permute-start | bytes 9437192 | tf_op jit(solution)/shard_map/ppermute | solution.py:24
  1.2 14.5 %collective-permute-start.2 = (bf16[384,4096]{1,0:T(8,128)(2,1)}, bf16[384,4096]{1,0:T(8,128)(2,1)}, u32[]{:S(2)}, u32[]{:S(2)}) collective-permute-start(bf16[384,4096]{1,0:T(8,128)(2,1)} %bitcast.30), channel_id=1, source_target_pairs={{0,1},{1,0},{2,3},{3,2},{4,5},{5,4},{6,7},{7,6},{8,9},{9,8},{10,11... | collective-permute-start | bytes 9437192 | tf_op jit(solution)/shard_map/ppermute | solution.py:24
  2.8 0.7 copy-start.2
  3.5 1.2 copy-start.6
  4.7 1.2 copy-start.7
  10.3 87.3 %copy-start.8 = (bf16[4096,384]{1,0:T(8,128)(2,1)}, bf16[4096,384]{1,0:T(8,128)(2,1)S(1)}, u32[]{:S(2)}) copy-start(bf16[4096,384]{1,0:T(8,128)(2,1)S(1)} %collective-permute-done.gs) | copy-start | bytes 9437188
  15.7 81.8 %copy-start.3 = (bf16[1,1,4096,384]{3,2,1,0:T(8,128)(2,1)S(1)}, bf16[1,1,4096,384]{3,2,1,0:T(8,128)(2,1)}, u32[]{:S(2)}) copy-start(bf16[1,1,4096,384]{3,2,1,0:T(8,128)(2,1)} %param.11) | copy-start | bytes 9437188
  15.7 81.8 %copy-start.4 = (bf16[1,1,4096,384]{3,2,1,0:T(8,128)(2,1)S(1)}, bf16[1,1,4096,384]{3,2,1,0:T(8,128)(2,1)}, u32[]{:S(2)}) copy-start(bf16[1,1,4096,384]{3,2,1,0:T(8,128)(2,1)} %param.12) | copy-start | bytes 9437188
  15.7 81.8 %copy-start.5 = (bf16[1,1,384,4096]{3,2,1,0:T(8,128)(2,1)S(1)}, bf16[1,1,384,4096]{3,2,1,0:T(8,128)(2,1)}, u32[]{:S(2)}) copy-start(bf16[1,1,384,4096]{3,2,1,0:T(8,128)(2,1)} %param.13) | copy-start | bytes 9437188
  116.6 1.0 copy-start
  117.6 0.8 copy-start.1
  118.4 36.9 %all-to-all-start.1 = ((bf16[16,24,3072]{2,1,0:T(8,128)(2,1)}), bf16[16,24,3072]{2,1,0:T(8,128)(2,1)S(1)}, u32[]{:S(2)}, u32[]{:S(2)}) async-start(bf16[16,24,3072]{2,1,0:T(8,128)(2,1)} %bitcast.10), calls=%async_computation.1 | async-start | bytes 4718592 | tf_op jit(solution)/shard_map/all_to_all | solution.py:28
  132.9 40.6 %collective-permute-start.4 = (bf16[4096,384]{1,0:T(8,128)(2,1)}, bf16[4096,384]{1,0:T(8,128)(2,1)}, u32[]{:S(2)}, u32[]{:S(2)}) collective-permute-start(bf16[4096,384]{1,0:T(8,128)(2,1)} %get-tuple-element.42), channel_id=1, source_target_pairs={{0,1},{1,0},{2,3},{3,2},{4,5},{5,4},{6,7},{7,6},{8,9},{9,8},{10,11... | collective-permute-start | bytes 9437192 | tf_op jit(solution)/shard_map/ppermute | solution.py:24
  133.0 40.6 %collective-permute-start.5 = (bf16[4096,384]{1,0:T(8,128)(2,1)}, bf16[4096,384]{1,0:T(8,128)(2,1)}, u32[]{:S(2)}, u32[]{:S(2)}) collective-permute-start(bf16[4096,384]{1,0:T(8,128)(2,1)} %get-tuple-element.43), channel_id=1, source_target_pairs={{0,1},{1,0},{2,3},{3,2},{4,5},{5,4},{6,7},{7,6},{8,9},{9,8},{10,11... | collective-permute-start | bytes 9437192 | tf_op jit(solution)/shard_map/ppermute | solution.py:24
  133.5 40.1 %collective-permute-start.6 = (bf16[384,4096]{1,0:T(8,128)(2,1)}, bf16[384,4096]{1,0:T(8,128)(2,1)}, u32[]{:S(2)}, u32[]{:S(2)}) collective-permute-start(bf16[384,4096]{1,0:T(8,128)(2,1)} %get-tuple-element.44), channel_id=1, source_target_pairs={{0,1},{1,0},{2,3},{3,2},{4,5},{5,4},{6,7},{7,6},{8,9},{9,8},{10,11... | collective-permute-start | bytes 9437192 | tf_op jit(solution)/shard_map/ppermute | solution.py:24
  155.4 17.8 %all-to-all-start.2 = ((bf16[16,24,1024]{2,1,0:T(8,128)(2,1)}), bf16[16,24,1024]{2,1,0:T(8,128)(2,1)S(1)}, u32[]{:S(2)}, u32[]{:S(2)}) async-start(bf16[16,24,1024]{2,1,0:T(8,128)(2,1)} %bitcast.12), calls=%async_computation.2 | async-start | bytes 1572864 | tf_op jit(solution)/shard_map/all_to_all | solution.py:28
  160.5 27.4 %collective-permute-start.3 = (bf16[128,3072]{1,0:T(8,128)(2,1)}, bf16[128,3072]{1,0:T(8,128)(2,1)S(1)}, u32[]{:S(2)}, u32[]{:S(2)}) collective-permute-start(bf16[128,3072]{1,0:T(8,128)(2,1)} %convolution_convert_fusion), channel_id=1, source_target_pairs={{0,96},{32,0},{64,32},{96,64},{1,97},{33,1},{65,33},{97,65},{2,98}... | collective-permute-start | bytes 2359304 | tf_op jit(solution)/shard_map/ppermute | solution.py:284
  187.1 7.6 %collective-permute-start.7 = (bf16[128,1024]{1,0:T(8,128)(2,1)S(1)}, bf16[128,1024]{1,0:T(8,128)(2,1)S(1)}, u32[]{:S(2)}, u32[]{:S(2)}) collective-permute-start(bf16[128,1024]{1,0:T(8,128)(2,1)S(1)} %convolution_convert_fusion.1), channel_id=1, source_target_pairs={{0,96},{32,0},{64,32},{96,64},{1,97},{33,1},{65,33},{97,65},{2,98}... | collective-permute-start | bytes 786440 | tf_op jit(solution)/shard_map/ppermute | solution.py:284

commit v4 on v3

--- a/solution.py
+++ b/solution.py
@@ -102,17 +102,16 @@
         out_shape=[jax.ShapeDtypeStruct((count, 2 * width), jnp.bfloat16) for count in slots]
         + [jax.ShapeDtypeStruct((tokens, count), jnp.bfloat16) for count in slots],
         scratch_shapes=[pltpu.VMEM((count, tokens), jnp.bfloat16) for count in slots],
-        compiler_params=pltpu.CompilerParams(vmem_limit_bytes=16 * MIB),
+        compiler_params=pltpu.CompilerParams(vmem_limit_bytes=LIMIT),
         cost_estimate=cost(4 * sum(slots) * tokens * width, 6 * sum(slots) * width),
         name="deal_rows",
     )(ids.reshape(1, tokens), ids, gates, stash, out_grad)
     return outs[: len(chunks)], outs[len(chunks) :]
 
 
-def middle_kernel(steps, cuts, rows_ref, go, uo, do, gs, us, ds, *refs):
-    backs, refs = refs[: len(cuts)], refs[len(cuts) :]
+def middle_kernel(steps, rows_ref, go, uo, do, gs, us, ds, back, *refs):
     hidden, deltas, held, joined, down, pre, tail, out, sems, out_sems = refs
-    rows, width = out.shape
+    rows, width = held.shape[0], held.shape[1] // 2
     units = go.shape[1]
     span = width // steps
 
@@ -165,40 +164,31 @@
             ).astype(jnp.bfloat16)
             deltas[at, up] = (grad * silu_a).astype(jnp.bfloat16)
 
-    def leave(back, k, begin):
-        return pltpu.make_async_copy(out.at[:, block(k)], back.at[:, block(k - begin)], out_sems.at[k])
-
-    begin = 0
-    ranges = []
-    for back, cut in zip(backs, cuts):
-        ranges.append((back, begin, begin + cut // span))
-        begin += cut // span
-    for back, begin, end in ranges:
-
-        @pl.loop(begin, end)
-        def _(k):
-            out[:, block(k)] = dot(deltas[...], joined[block(k), :], NEXT_LAST).astype(jnp.bfloat16)
-            leave(back, k, begin).start()
-
-    for back, begin, end in ranges:
-
-        @pl.loop(begin, end)
-        def _(k):
-            leave(back, k, begin).wait()
-
-
-def middle(rows, own, sibling, cuts):
+    def leave(k):
+        return pltpu.make_async_copy(out.at[:, block(k)], back.at[:, block(k)], out_sems.at[k])
+
+    @pl.loop(0, back.shape[1] // span)
+    def _(k):
+        out[:, block(k)] = dot(deltas[...], joined[block(k), :], NEXT_LAST).astype(jnp.bfloat16)
+        leave(k).start()
+
+    @pl.loop(0, back.shape[1] // span)
+    def _(k):
+        leave(k).wait()
+
+
+def middle(rows, own, sibling, cut):
     count, width = rows.shape[0], rows.shape[1] // 2
     units = own[0].shape[1]
     steps = 8
     anywhere = pl.BlockSpec(memory_space=pl.ANY)
     whole = pl.BlockSpec(memory_space=pltpu.VMEM)
-    outs = pl.pallas_call(
-        functools.partial(middle_kernel, steps, cuts),
+    return pl.pallas_call(
+        functools.partial(middle_kernel, steps),
         in_specs=[anywhere] * 7,
-        out_specs=[anywhere] * len(cuts) + [whole] * 2,
-        out_shape=[jax.ShapeDtypeStruct((count, cut), jnp.bfloat16) for cut in cuts]
-        + [
+        out_specs=[anywhere] + [whole] * 2,
+        out_shape=[
+            jax.ShapeDtypeStruct((count, cut), jnp.bfloat16),
             jax.ShapeDtypeStruct((count, CORES * units), jnp.bfloat16),
             jax.ShapeDtypeStruct((count, 2 * CORES * units), jnp.bfloat16),
         ],
@@ -208,15 +198,65 @@
             pltpu.VMEM((CORES * units, width), jnp.bfloat16),
             pltpu.VMEM((count, 2 * CORES * units), jnp.float32),
             pltpu.VMEM((count, CORES * units), jnp.float32),
-            pltpu.VMEM((count, width), jnp.bfloat16),
+            pltpu.VMEM((count, cut), jnp.bfloat16),
             pltpu.SemaphoreType.DMA((8, steps)),
             pltpu.SemaphoreType.DMA((steps,)),
         ],
-        compiler_params=pltpu.CompilerParams(vmem_limit_bytes=40 * MIB),
-        cost_estimate=cost(10 * count * width * CORES * units, 30 * MIB),
+        compiler_params=pltpu.CompilerParams(vmem_limit_bytes=LIMIT),
+        cost_estimate=cost(8 * count * width * CORES * units, 30 * MIB),
         name="middle",
     )(rows, *own, *sibling)
-    return outs[: len(cuts)], outs[-2], outs[-1]
+
+
+def rest_kernel(deltas, *refs):
+    weights, back = refs[:-1], refs[-1]
+    units = weights[0].shape[1]
+    total = dot(deltas[:, :units], weights[0][...], NEXT_LAST)
+    for i, weight in enumerate(weights[1:], 1):
+        total += dot(deltas[:, i * units : (i + 1) * units], weight[...], NEXT_LAST)
+    back[...] = total.astype(jnp.bfloat16)
+
+
+def rest(deltas, own, sibling, cut):
+    count = deltas.shape[0]
+    width, units = own[0].shape
+    span = width // 8
+    first = cut // span
+    return pl.pallas_call(
+        rest_kernel,
+        grid=(width // span - first,),
+        in_specs=[pl.BlockSpec(deltas.shape, lambda i: (0, 0))]
+        + [pl.BlockSpec((span, units), lambda i: (i + first, 0))] * 4,
+        out_specs=pl.BlockSpec((count, span), lambda i: (0, i)),
+        out_shape=jax.ShapeDtypeStruct((count, width - cut), jnp.bfloat16),
+        compiler_params=pltpu.CompilerParams(vmem_limit_bytes=LIMIT),
+        cost_estimate=cost(8 * count * (width - cut) * units, 8 * MIB),
+        name="last_columns",
+    )(deltas, *own[:2], *sibling[:2])
+
+
+def combine_kernel(place_back, returned, mark, out):
+    out[...] = dot(place_back[...], returned[...]).astype(jnp.bfloat16)
+
+
+def combine(place_back, returned, mark):
+    tokens, slots = place_back.shape
+    width = returned.shape[1]
+    span = width // 3
+    return pl.pallas_call(
+        combine_kernel,
+        grid=(width // span,),
+        in_specs=[
+            pl.BlockSpec((tokens, slots), lambda i: (0, 0)),
+            pl.BlockSpec((slots, span), lambda i: (0, i)),
+            pl.BlockSpec(memory_space=pl.ANY),
+        ],
+        out_specs=pl.BlockSpec((tokens, span), lambda i: (0, i)),
+        out_shape=jax.ShapeDtypeStruct((tokens, width), jnp.bfloat16),
+        compiler_params=pltpu.CompilerParams(vmem_limit_bytes=LIMIT),
+        cost_estimate=cost(2 * tokens * slots * width, 2 * slots * width),
+        name="combine",
+    )(place_back, returned, mark)
 
 
 def grads_kernel(number, added, *refs):
@@ -275,26 +315,24 @@
     dealt, sibling = lax.optimization_barrier((dealt, sibling))
     rows = over_chips(dealt)
     width = stash.shape[2]
-    backs, hidden, deltas = middle(rows, own, sibling, (width * 3 // 4, width // 4))
+    cut = width * 5 // 8
+    back, hidden, deltas = middle(rows, own, sibling, cut)
+    last = rest(deltas, own, sibling, cut)
     theirs = weight_grads([rows], [hidden], [deltas], 1)
     received = tuple(swap_cores(part) for part in theirs)
 
-    def shift(returned):
-        input_grad = dot(place_back, returned).astype(jnp.bfloat16)
-        return input_grad, lambda value: lax.ppermute(
-            value, "section", [(i, (i - 1) % sections) for i in range(sections)]
-        )
-
-    first = over_chips(backs[0])
-    last, first = lax.optimization_barrier((backs[1], first))
+    def shift(value):
+        return lax.ppermute(value, "section", [(i, (i - 1) % sections) for i in range(sections)])
+
+    first = over_chips(back)
+    last, first = lax.optimization_barrier((last, first))
     last = over_chips(last)
-    first, move = shift(first)
+    first = dot(place_back, first).astype(jnp.bfloat16)
     deltas, first = lax.optimization_barrier((deltas, first))
-    first = move(first)
+    first = shift(first)
     grads = weight_grads([rows], [hidden], [deltas], 0, received)
-    last, move = shift(last)
-    last, grads = lax.optimization_barrier((last, tuple(grads)))
-    last = move(last)
+    mark = swap_cores(grads[0][:16, :128])
+    last = shift(combine(place_back, last, mark))
     prev_grad = jnp.concatenate([first, last], axis=1)
     return (prev_grad[None],) + tuple(grad[None, None] for grad in grads)
 

time: 196 us -> 204 us (1.041)
  Pallas kernels: 47.7 us -> 60.3 us
  waiting for transfers between devices: 46 us -> 42.2 us
    pallas_call x1 -> x3, Pallas kernels: 19 us -> 27.6 us  [the longest x1 18.1 us: middle(): pl.pallas_call(functools.partial(middle_kernel, steps), in_specs=[anywher...]
    all_to_all x2, waiting for transfers between devices: 33.8 us -> 29.3 us  [over_chips(): lax.all_to_all(value, 'chip', split_axis=0, concat_axis=0, tiled=True)]
    pallas_call x1, Pallas kernels: 4.34 us -> 8.31 us  [deal(): pl.pallas_call(functools.partial(deal_kernel, experts, chunks, blocks), g...]
    unnamed x18 -> x8, local copies, waits for them, and re-layouts: 4.97 us -> 1.05 us
    ppermute x2, waiting for transfers between devices: 6.85 us -> 9.65 us  [shift(): lax.ppermute(value, 'section', [(i, (i - 1) % sections) for i in range(se...]
    ppermute x6 -> x7, waiting for transfers between devices: 5.41 us -> 3.29 us  [swap_cores(): return lax.ppermute(value, 'core', [(0, 1), (1, 0)])]
  transfers between devices with their start and end apart: 10 -> 11, of which waited for: 5 -> 4; matrix products, arithmetic and copies ran while one was open for 2% -> 2% of each run, Pallas kernels for 15% -> 15%
where the time goes in v4:
time: 204 us; the launch traced here: 202 us
  blocking collectives  81.8 us (40%)
  Pallas kernels  60.3 us (30%)
  waiting for transfers between devices  42.2 us (21%)
  starting transfers between devices  10.3 us (5%)
  local copies, waits for them, and re-layouts  4.52 us (2%)
    all_to_all x1, blocking collectives, over_chips(): lax.all_to_all(value, 'chip', split_axis=0, concat_axis=0, tiled=True)  81.8 us
    all_to_all x2, waiting for transfers between devices, over_chips(): lax.all_to_all(value, 'chip', split_axis=0, concat_axis=0, tiled=True)  29.3 us
    pallas_call x2, Pallas kernels, weight_grads(): pl.pallas_call(functools.partial(grads_kernel, len(rows), len(received) >...  24.4 us
    pallas_call x1, Pallas kernels, middle(): pl.pallas_call(functools.partial(middle_kernel, steps), in_specs=[anywher...  18.1 us
    ppermute x2, waiting for transfers between devices, shift(): lax.ppermute(value, 'section', [(i, (i - 1) % sections) for i in range(se...  9.65 us
    pallas_call x1, Pallas kernels, deal(): pl.pallas_call(functools.partial(deal_kernel, experts, chunks, blocks), g...  8.31 us
    all_to_all x2, starting transfers between devices, over_chips(): lax.all_to_all(value, 'chip', split_axis=0, concat_axis=0, tiled=True)  7.41 us
    pallas_call x1, Pallas kernels, rest(): pl.pallas_call(rest_kernel, grid=(width // span - first,), in_specs=[pl.B...  6.27 us
  transfers between devices with their start and end apart: 11, of which 4 were waited for; matrix products, arithmetic and copies ran while one was open for 2% of the time, Pallas kernels for 15%

profile of v4, /device:TPU:6, one launch (start us, length us, event | category | flops | bytes accessed | tf_op | source)
XLA Modules:
  0.0 202.3 jit_solution(7964351877786061762)
XLA Ops:
  0.6 0.1 collective-permute-start
  0.7 0.5 collective-permute-start.1
  1.2 0.1 collective-permute-start.2
  1.3 1.4 copy.12.gates
  2.7 1.4 copy.11.col_ids
  4.1 8.3 %deal_rows.1 = (bf16[384,8192]{1,0:T(8,128)(2,1)}, bf16[128,384]{1,0:T(8,128)(2,1)}) custom-call(s32[1,128]{1,0:T(1,128)} %bitcast.39, s32[128,1]{1,0:T(8,128)} %copy.11.col_ids, f32[128,1]{1,0:T(8,128)} %copy.12.gates, bf16[128,4096]{1,0:T(8,128)(2,1)} %bitcast.45, bf16[128,4096]{1,0:T(8,128)(2,1)} %bitcast.46), custom_call_target="tpu_custom_call" | custom-call | flops 805306368 | bytes 9437184 | tf_op jit(solution)/shard_map/deal_rows/pallas_call | solution.py:90
  12.4 0.0 collective-permute-done.gs.refs_2_
  12.4 0.0 copy-start.1
  12.4 0.0 collective-permute-done.1.us.refs_3_
  12.4 3.3 %collective-permute-done.2.ds = bf16[384,4096]{1,0:T(8,128)(2,1)} collective-permute-done((bf16[384,4096]{1,0:T(8,128)(2,1)}, bf16[384,4096]{1,0:T(8,128)(2,1)}, u32[]{:S(2)}, u32[]{:S(2)}) %collective-permute-start.2) | collective-permute-done | bytes 3145760 | tf_op jit(solution)/shard_map/ppermute | solution.py:24
  15.7 81.8 %all_to_all.34 = bf16[16,24,8192]{2,1,0:T(8,128)(2,1)} all-to-all(bf16[16,24,8192]{2,1,0:T(8,128)(2,1)} %bitcast.27), channel_id=1, replica_groups=mesh['section'=4,'chip'=16,'core'=2] {'chip'}, dimensions={0} | all-to-all | bytes 12582912 | tf_op jit(solution)/shard_map/all_to_all | solution.py:28
  97.5 0.0 copy-done.1
  97.5 18.1 %middle.1 = (bf16[384,2560]{1,0:T(8,128)(2,1)}, bf16[384,768]{1,0:T(8,128)(2,1)}, bf16[384,1536]{1,0:T(8,128)(2,1)}) custom-call(bf16[384,8192]{1,0:T(8,128)(2,1)} %bitcast.21, bf16[4096,384]{1,0:T(8,128)(2,1)} %bitcast.31, bf16[4096,384]{1,0:T(8,128)(2,1)} %bitcast.34, bf16[384,4096]{1,0:T(8,128)(2,1)} %bitcast.42, bf16[4096,384]{1,0:T(8,128)(2,1)} %copy-done.1, ...), custom_call_target="tpu_custom_call" | custom-call | flops 9663676416 | bytes 31457280 | tf_op jit(solution)/shard_map/middle/pallas_call | solution.py:186
  115.6 10.8 %sibling_grads.1 = (bf16[4096,384]{1,0:T(8,128)(2,1)}, bf16[4096,384]{1,0:T(8,128)(2,1)}, bf16[384,4096]{1,0:T(8,128)(2,1)}) custom-call(bf16[384,8192]{1,0:T(8,128)(2,1)} %bitcast.22, bf16[384,8192]{1,0:T(8,128)(2,1)} %bitcast.23, bf16[384,768]{1,0:T(8,128)(2,1)} %get-tuple-element.34.refs_2_, bf16[384,1536]{1,0:T(8,128)(2,1)} %get-tuple-element.35.deltas.refs_3_), custom_call_target="tpu_custom_call" | custom-call | flops 3623878656 | bytes 16777216 | tf_op jit(solution)/shard_map/sibling_grads/pallas_call | solution.py:284
  126.5 0.0 collective-permute-start.4
  126.5 0.5 collective-permute-start.5
  127.0 0.1 collective-permute-start.6
  127.0 3.7 %all-to-all-start.1 = ((bf16[16,24,2560]{2,1,0:T(8,128)(2,1)}), bf16[16,24,2560]{2,1,0:T(8,128)(2,1)S(1)}, u32[]{:S(2)}, u32[]{:S(2)}) async-start(bf16[16,24,2560]{2,1,0:T(8,128)(2,1)} %bitcast.36), calls=%async_computation.1 | async-start | bytes 3932160 | tf_op jit(solution)/shard_map/all_to_all | solution.py:28
  130.8 0.0 copy-start.2
  130.8 6.3 %last_columns.1 = bf16[384,1536]{1,0:T(8,128)(2,1)} custom-call(bf16[384,1536]{1,0:T(8,128)(2,1)} %get-tuple-element.35.deltas.refs_3_, bf16[4096,384]{1,0:T(8,128)(2,1)} %bitcast.32, bf16[4096,384]{1,0:T(8,128)(2,1)} %bitcast.35, bf16[4096,384]{1,0:T(8,128)(2,1)} %copy-done.1, bf16[4096,384]{1,0:T(8,128)(2,1)} %collective-permute-done.1.us.refs_3_), custom_call_target="tpu_custom_call" | custom-call | flops 1811939328 | bytes 8388608 | tf_op jit(solution)/shard_map/last_columns/pallas_call | solution.py:225
  137.0 26.4 %all-to-all-done.1 = bf16[16,24,2560]{2,1,0:T(8,128)(2,1)S(1)} async-done(((bf16[16,24,2560]{2,1,0:T(8,128)(2,1)}), bf16[16,24,2560]{2,1,0:T(8,128)(2,1)S(1)}, u32[]{:S(2)}, u32[]{:S(2)}) %all-to-all-start.1) | async-done | bytes 1966112 | tf_op jit(solution)/shard_map/all_to_all | solution.py:28
  163.5 3.7 %all-to-all-start.2 = ((bf16[16,24,1536]{2,1,0:T(8,128)(2,1)}), bf16[16,24,1536]{2,1,0:T(8,128)(2,1)S(1)}, u32[]{:S(2)}, u32[]{:S(2)}) async-start(bf16[16,24,1536]{2,1,0:T(8,128)(2,1)} %bitcast.28), calls=%async_computation.2 | async-start | bytes 2359296 | tf_op jit(solution)/shard_map/all_to_all | solution.py:28
  167.2 0.0 copy-done.2
  167.2 1.3 convolution_convert_fusion
  168.5 0.8 collective-permute-start.3
  169.3 0.0 collective-permute-done.4.refs_4_
  169.3 0.0 collective-permute-done.5.refs_5_
  169.3 0.0 collective-permute-done.6.refs_6_
  169.4 13.6 %own_grads.1 = (bf16[4096,384]{1,0:T(8,128)(2,1)}, bf16[4096,384]{1,0:T(8,128)(2,1)}, bf16[384,4096]{1,0:T(8,128)(2,1)}) custom-call(bf16[384,8192]{1,0:T(8,128)(2,1)} %bitcast.24, bf16[384,8192]{1,0:T(8,128)(2,1)} %bitcast.25, bf16[384,768]{1,0:T(8,128)(2,1)} %get-tuple-element.34.refs_2_, bf16[384,1536]{1,0:T(8,128)(2,1)} %get-tuple-element.35.deltas.refs_3_, ...), custom_call_target="tpu_custom_call" | custom-call | flops 3623878656 | bytes 16777216 | tf_op jit(solution)/shard_map/own_grads/pallas_call | solution.py:284
  182.9 0.7 slice.3
  183.6 0.0 collective-permute-start.7
  183.6 2.8 %all-to-all-done.2 = bf16[16,24,1536]{2,1,0:T(8,128)(2,1)S(1)} async-done(((bf16[16,24,1536]{2,1,0:T(8,128)(2,1)}), bf16[16,24,1536]{2,1,0:T(8,128)(2,1)S(1)}, u32[]{:S(2)}, u32[]{:S(2)}) %all-to-all-start.2) | async-done | bytes 1179680 | tf_op jit(solution)/shard_map/all_to_all | solution.py:28
  186.5 0.0 copy-start
  186.5 0.0 collective-permute-done.7.mark
  186.5 0.0 copy-start.3
  186.5 1.0 copy-done
  187.5 0.0 copy-done.3
  187.5 3.2 %combine.1 = bf16[128,1536]{1,0:T(8,128)(2,1)} custom-call(bf16[128,384]{1,0:T(8,128)(2,1)} %get-tuple-element.29.place_back, bf16[384,1536]{1,0:T(8,128)(2,1)} %bitcast.29, bf16[16,128]{1,0:T(8,128)(2,1)} %copy-done.3), custom_call_target="tpu_custom_call" | custom-call | flops 150994944 | bytes 1179648 | tf_op jit(solution)/shard_map/combine/pallas_call | solution.py:246
  190.7 0.8 collective-permute-start.8
  191.5 0.0 collective-permute-done.3
  191.5 9.6 %collective-permute-done.8 = bf16[128,1536]{1,0:T(8,128)(2,1)S(1)} collective-permute-done((bf16[128,1536]{1,0:T(8,128)(2,1)}, bf16[128,1536]{1,0:T(8,128)(2,1)S(1)}, u32[]{:S(2)}, u32[]{:S(2)}) %collective-permute-start.8) | collective-permute-done | bytes 393248 | tf_op jit(solution)/shard_map/ppermute | solution.py:325
  201.2 1.1 maximum_bitcast_fusion
Async XLA Ops:
  0.6 11.8 %collective-permute-start = (bf16[4096,384]{1,0:T(8,128)(2,1)}, bf16[4096,384]{1,0:T(8,128)(2,1)S(1)}, u32[]{:S(2)}, u32[]{:S(2)}) collective-permute-start(bf16[4096,384]{1,0:T(8,128)(2,1)} %bitcast.30), channel_id=1, source_target_pairs={{0,1},{1,0},{2,3},{3,2},{4,5},{5,4},{6,7},{7,6},{8,9},{9,8},{10,11... | collective-permute-start | bytes 9437192 | tf_op jit(solution)/shard_map/ppermute | solution.py:24
  0.7 11.7 %collective-permute-start.1 = (bf16[4096,384]{1,0:T(8,128)(2,1)}, bf16[4096,384]{1,0:T(8,128)(2,1)}, u32[]{:S(2)}, u32[]{:S(2)}) collective-permute-start(bf16[4096,384]{1,0:T(8,128)(2,1)} %bitcast.33), channel_id=1, source_target_pairs={{0,1},{1,0},{2,3},{3,2},{4,5},{5,4},{6,7},{7,6},{8,9},{9,8},{10,11... | collective-permute-start | bytes 9437192 | tf_op jit(solution)/shard_map/ppermute | solution.py:24
  1.2 14.5 %collective-permute-start.2 = (bf16[384,4096]{1,0:T(8,128)(2,1)}, bf16[384,4096]{1,0:T(8,128)(2,1)}, u32[]{:S(2)}, u32[]{:S(2)}) collective-permute-start(bf16[384,4096]{1,0:T(8,128)(2,1)} %bitcast.41), channel_id=1, source_target_pairs={{0,1},{1,0},{2,3},{3,2},{4,5},{5,4},{6,7},{7,6},{8,9},{9,8},{10,11... | collective-permute-start | bytes 9437192 | tf_op jit(solution)/shard_map/ppermute | solution.py:24
  12.4 85.1 %copy-start.1 = (bf16[4096,384]{1,0:T(8,128)(2,1)}, bf16[4096,384]{1,0:T(8,128)(2,1)S(1)}, u32[]{:S(2)}) copy-start(bf16[4096,384]{1,0:T(8,128)(2,1)S(1)} %collective-permute-done.gs.refs_2_) | copy-start | bytes 9437188
  126.5 42.9 %collective-permute-start.4 = (bf16[4096,384]{1,0:T(8,128)(2,1)}, bf16[4096,384]{1,0:T(8,128)(2,1)}, u32[]{:S(2)}, u32[]{:S(2)}) collective-permute-start(bf16[4096,384]{1,0:T(8,128)(2,1)} %get-tuple-element.36), channel_id=1, source_target_pairs={{0,1},{1,0},{2,3},{3,2},{4,5},{5,4},{6,7},{7,6},{8,9},{9,8},{10,11... | collective-permute-start | bytes 9437192 | tf_op jit(solution)/shard_map/ppermute | solution.py:24
  126.5 42.9 %collective-permute-start.5 = (bf16[4096,384]{1,0:T(8,128)(2,1)}, bf16[4096,384]{1,0:T(8,128)(2,1)}, u32[]{:S(2)}, u32[]{:S(2)}) collective-permute-start(bf16[4096,384]{1,0:T(8,128)(2,1)} %get-tuple-element.37), channel_id=1, source_target_pairs={{0,1},{1,0},{2,3},{3,2},{4,5},{5,4},{6,7},{7,6},{8,9},{9,8},{10,11... | collective-permute-start | bytes 9437192 | tf_op jit(solution)/shard_map/ppermute | solution.py:24
  127.0 42.4 %collective-permute-start.6 = (bf16[384,4096]{1,0:T(8,128)(2,1)}, bf16[384,4096]{1,0:T(8,128)(2,1)}, u32[]{:S(2)}, u32[]{:S(2)}) collective-permute-start(bf16[384,4096]{1,0:T(8,128)(2,1)} %get-tuple-element.38), channel_id=1, source_target_pairs={{0,1},{1,0},{2,3},{3,2},{4,5},{5,4},{6,7},{7,6},{8,9},{9,8},{10,11... | collective-permute-start | bytes 9437192 | tf_op jit(solution)/shard_map/ppermute | solution.py:24
  127.0 36.4 %all-to-all-start.1 = ((bf16[16,24,2560]{2,1,0:T(8,128)(2,1)}), bf16[16,24,2560]{2,1,0:T(8,128)(2,1)S(1)}, u32[]{:S(2)}, u32[]{:S(2)}) async-start(bf16[16,24,2560]{2,1,0:T(8,128)(2,1)} %bitcast.36), calls=%async_computation.1 | async-start | bytes 3932160 | tf_op jit(solution)/shard_map/all_to_all | solution.py:28
  130.8 36.4 %copy-start.2 = (bf16[128,384]{1,0:T(8,128)(2,1)S(1)}, bf16[128,384]{1,0:T(8,128)(2,1)}, u32[]{:S(2)}) copy-start(bf16[128,384]{1,0:T(8,128)(2,1)} %get-tuple-element.29.place_back) | copy-start | bytes 294916
  163.5 23.0 %all-to-all-start.2 = ((bf16[16,24,1536]{2,1,0:T(8,128)(2,1)}), bf16[16,24,1536]{2,1,0:T(8,128)(2,1)S(1)}, u32[]{:S(2)}, u32[]{:S(2)}) async-start(bf16[16,24,1536]{2,1,0:T(8,128)(2,1)} %bitcast.28), calls=%async_computation.2 | async-start | bytes 2359296 | tf_op jit(solution)/shard_map/all_to_all | solution.py:28
  168.5 23.0 %collective-permute-start.3 = (bf16[128,2560]{1,0:T(8,128)(2,1)}, bf16[128,2560]{1,0:T(8,128)(2,1)S(1)}, u32[]{:S(2)}, u32[]{:S(2)}) collective-permute-start(bf16[128,2560]{1,0:T(8,128)(2,1)} %convolution_convert_fusion), channel_id=1, source_target_pairs={{0,96},{32,0},{64,32},{96,64},{1,97},{33,1},{65,33},{97,65},{2,98}... | collective-permute-start | bytes 1966088 | tf_op jit(solution)/shard_map/ppermute | solution.py:325
  183.6 2.9 %collective-permute-start.7 = (bf16[16,128]{1,0:T(8,128)(2,1)S(1)}, bf16[16,128]{1,0:T(8,128)(2,1)S(1)}, u32[]{:S(2)}, u32[]{:S(2)}) collective-permute-start(bf16[16,128]{1,0:T(8,128)(2,1)S(1)} %slice.3), channel_id=1, source_target_pairs={{0,1},{1,0},{2,3},{3,2},{4,5},{5,4},{6,7},{7,6},{8,9},{9,8},{10,11... | collective-permute-start | bytes 12296 | tf_op jit(solution)/shard_map/ppermute | solution.py:24
  186.5 1.0 copy-start
  186.5 1.0 copy-start.3
  190.7 10.5 %collective-permute-start.8 = (bf16[128,1536]{1,0:T(8,128)(2,1)}, bf16[128,1536]{1,0:T(8,128)(2,1)S(1)}, u32[]{:S(2)}, u32[]{:S(2)}) collective-permute-start(bf16[128,1536]{1,0:T(8,128)(2,1)} %combine.1), channel_id=1, source_target_pairs={{0,96},{32,0},{64,32},{96,64},{1,97},{33,1},{65,33},{97,65},{2,98}... | collective-permute-start | bytes 1179656 | tf_op jit(solution)/shard_map/ppermute | solution.py:325

commit v5 on v3

--- a/solution.py
+++ b/solution.py
@@ -212,11 +212,35 @@
             pltpu.SemaphoreType.DMA((8, steps)),
             pltpu.SemaphoreType.DMA((steps,)),
         ],
-        compiler_params=pltpu.CompilerParams(vmem_limit_bytes=40 * MIB),
+        compiler_params=pltpu.CompilerParams(vmem_limit_bytes=LIMIT),
         cost_estimate=cost(10 * count * width * CORES * units, 30 * MIB),
         name="middle",
     )(rows, *own, *sibling)
     return outs[: len(cuts)], outs[-2], outs[-1]
+
+
+def combine_kernel(place_back, returned, mark, out):
+    out[...] = dot(place_back[...], returned[...]).astype(jnp.bfloat16)
+
+
+def combine(place_back, returned, mark):
+    tokens, slots = place_back.shape
+    width = returned.shape[1]
+    span = width // 3
+    return pl.pallas_call(
+        combine_kernel,
+        grid=(width // span,),
+        in_specs=[
+            pl.BlockSpec((tokens, slots), lambda i: (0, 0)),
+            pl.BlockSpec((slots, span), lambda i: (0, i)),
+            pl.BlockSpec(memory_space=pl.ANY),
+        ],
+        out_specs=pl.BlockSpec((tokens, span), lambda i: (0, i)),
+        out_shape=jax.ShapeDtypeStruct((tokens, width), jnp.bfloat16),
+        compiler_params=pltpu.CompilerParams(vmem_limit_bytes=LIMIT),
+        cost_estimate=cost(2 * tokens * slots * width, 2 * slots * width),
+        name="combine",
+    )(place_back, returned, mark)
 
 
 def grads_kernel(number, added, *refs):
@@ -275,26 +299,23 @@
     dealt, sibling = lax.optimization_barrier((dealt, sibling))
     rows = over_chips(dealt)
     width = stash.shape[2]
-    backs, hidden, deltas = middle(rows, own, sibling, (width * 3 // 4, width // 4))
+    cut = width * 5 // 8
+    backs, hidden, deltas = middle(rows, own, sibling, (cut, width - cut))
     theirs = weight_grads([rows], [hidden], [deltas], 1)
     received = tuple(swap_cores(part) for part in theirs)
 
-    def shift(returned):
-        input_grad = dot(place_back, returned).astype(jnp.bfloat16)
-        return input_grad, lambda value: lax.ppermute(
-            value, "section", [(i, (i - 1) % sections) for i in range(sections)]
-        )
+    def shift(value):
+        return lax.ppermute(value, "section", [(i, (i - 1) % sections) for i in range(sections)])
 
     first = over_chips(backs[0])
     last, first = lax.optimization_barrier((backs[1], first))
     last = over_chips(last)
-    first, move = shift(first)
+    first = dot(place_back, first).astype(jnp.bfloat16)
     deltas, first = lax.optimization_barrier((deltas, first))
-    first = move(first)
+    first = shift(first)
     grads = weight_grads([rows], [hidden], [deltas], 0, received)
-    last, move = shift(last)
-    last, grads = lax.optimization_barrier((last, tuple(grads)))
-    last = move(last)
+    mark = swap_cores(grads[0][:16, :128])
+    last = shift(combine(place_back, last, mark))
     prev_grad = jnp.concatenate([first, last], axis=1)
     return (prev_grad[None],) + tuple(grad[None, None] for grad in grads)
 

time: 196 us -> 201 us (1.026)
  blocking collectives: 81.8 us -> 112 us
  waiting for transfers between devices: 46 us -> 17.9 us
  Pallas kernels: 47.7 us -> 52.5 us
  starting transfers between devices: 10.1 us -> 6.58 us
    all_to_all x2 -> x1, waiting for transfers between devices: 33.8 us -> 2.12 us  [over_chips(): lax.all_to_all(value, 'chip', split_axis=0, concat_axis=0, tiled=True)]
    all_to_all x1 -> x2, blocking collectives: 81.8 us -> 112 us  [over_chips(): lax.all_to_all(value, 'chip', split_axis=0, concat_axis=0, tiled=True)]
    all_to_all x2 -> x1, starting transfers between devices: 7.34 us -> 3.7 us  [over_chips(): lax.all_to_all(value, 'chip', split_axis=0, concat_axis=0, tiled=True)]
    ppermute x2, waiting for transfers between devices: 6.85 us -> 10.4 us  [shift(): lax.ppermute(value, 'section', [(i, (i - 1) % sections) for i in range(se...]
    pallas_call x0 -> x1, Pallas kernels: none -> 3.18 us  [combine(): pl.pallas_call(combine_kernel, grid=(width // span,), in_specs=[pl.BlockS...]
    unnamed x18 -> x16, local copies, waits for them, and re-layouts: 4.97 us -> 4.15 us
    ppermute x6 -> x7, waiting for transfers between devices: 5.41 us -> 5.4 us  [swap_cores(): return lax.ppermute(value, 'core', [(0, 1), (1, 0)])]
  transfers between devices with their start and end apart: 10 -> 10, of which waited for: 5 -> 4; matrix products, arithmetic and copies ran while one was open for 2% -> 2% of each run, Pallas kernels for 15% -> 11%
where the time goes in v5:
time: 201 us; the launch traced here: 199 us
  blocking collectives  112 us (56%)
  Pallas kernels  52.5 us (26%)
  waiting for transfers between devices  17.9 us (9%)
  starting transfers between devices  6.58 us (3%)
  local copies, waits for them, and re-layouts  6.36 us (3%)
    all_to_all x2, blocking collectives, over_chips(): lax.all_to_all(value, 'chip', split_axis=0, concat_axis=0, tiled=True)  112 us
    pallas_call x2, Pallas kernels, weight_grads(): pl.pallas_call(functools.partial(grads_kernel, len(rows), len(received) >...  24.5 us
    pallas_call x1, Pallas kernels, middle(): pl.pallas_call(functools.partial(middle_kernel, steps, cuts), in_specs=[a...  20.5 us
    ppermute x2, waiting for transfers between devices, shift(): lax.ppermute(value, 'section', [(i, (i - 1) % sections) for i in range(se...  10.4 us
    ppermute x7, waiting for transfers between devices, swap_cores(): return lax.ppermute(value, 'core', [(0, 1), (1, 0)])  5.4 us
    pallas_call x1, Pallas kernels, deal(): pl.pallas_call(functools.partial(deal_kernel, experts, chunks, blocks), g...  4.34 us
    unnamed x16, local copies, waits for them, and re-layouts  4.15 us
  transfers between devices with their start and end apart: 10, of which 4 were waited for; matrix products, arithmetic and copies ran while one was open for 2% of the time, Pallas kernels for 11%

profile of v5, /device:TPU:6, one launch (start us, length us, event | category | flops | bytes accessed | tf_op | source)
XLA Modules:
  0.0 198.8 jit_solution(17597167994838825527)
XLA Ops:
  0.6 0.1 collective-permute-start
  0.7 0.5 collective-permute-start.1
  1.2 0.1 collective-permute-start.2
  1.3 0.8 copy.12.gates
  2.1 0.8 copy.11.col_ids
  2.8 0.0 copy-start.1
  2.8 0.6 copy-done.1
  3.5 0.0 copy-start.2
  3.5 1.2 copy-done.2
  4.7 0.0 copy-start.3
  4.7 1.2 copy-done.3
  5.9 4.3 %deal_rows.1 = (bf16[384,8192]{1,0:T(8,128)(2,1)S(1)}, bf16[128,384]{1,0:T(8,128)(2,1)S(1)}) custom-call(s32[1,128]{1,0:T(1,128)S(1)} %bitcast.23, s32[128,1]{1,0:T(8,128)S(1)} %copy.11.col_ids, f32[128,1]{1,0:T(8,128)S(1)} %copy.12.gates, bf16[128,4096]{1,0:T(8,128)(2,1)S(1)} %bitcast.24, bf16[128,4096]{1,0:T(8,128)(2,1)S(1)} %bitcast.25), custom_call_target="tpu_custom_call" | custom-call | flops 805306368 | bytes 9437184 | tf_op jit(solution)/shard_map/deal_rows/pallas_call | solution.py:90
  10.3 0.0 copy-start
  10.3 0.0 collective-permute-done.gs
  10.3 0.0 copy-start.7
  10.3 0.9 collective-permute-done.1.us
  11.2 4.5 %collective-permute-done.2.ds = bf16[384,4096]{1,0:T(8,128)(2,1)} collective-permute-done((bf16[384,4096]{1,0:T(8,128)(2,1)}, bf16[384,4096]{1,0:T(8,128)(2,1)}, u32[]{:S(2)}, u32[]{:S(2)}) %collective-permute-start.2) | collective-permute-done | bytes 3145760 | tf_op jit(solution)/shard_map/ppermute | solution.py:24
  15.7 81.6 %all_to_all.34 = bf16[16,24,8192]{2,1,0:T(8,128)(2,1)} all-to-all(bf16[16,24,8192]{2,1,0:T(8,128)(2,1)S(1)} %bitcast.21), channel_id=1, replica_groups=mesh['section'=4,'chip'=16,'core'=2] {'chip'}, dimensions={0} | all-to-all | bytes 12582912 | tf_op jit(solution)/shard_map/all_to_all | solution.py:28
  97.3 0.0 copy-done.7
  97.3 20.5 %middle.1 = (bf16[384,2560]{1,0:T(8,128)(2,1)}, bf16[384,1536]{1,0:T(8,128)(2,1)}, bf16[384,768]{1,0:T(8,128)(2,1)}, bf16[384,1536]{1,0:T(8,128)(2,1)}) custom-call(bf16[384,8192]{1,0:T(8,128)(2,1)} %bitcast.26, bf16[4096,384]{1,0:T(8,128)(2,1)} %bitcast.38, bf16[4096,384]{1,0:T(8,128)(2,1)} %bitcast.40, bf16[384,4096]{1,0:T(8,128)(2,1)} %bitcast.42, ...), custom_call_target="tpu_custom_call" | custom-call | flops 12079595520 | bytes 31457280 | tf_op jit(solution)/shard_map/middle/pallas_call | solution.py:196
  117.8 0.0 copy-start.5
  117.8 10.9 %sibling_grads.1 = (bf16[4096,384]{1,0:T(8,128)(2,1)}, bf16[4096,384]{1,0:T(8,128)(2,1)}, bf16[384,4096]{1,0:T(8,128)(2,1)}) custom-call(bf16[384,8192]{1,0:T(8,128)(2,1)} %bitcast.27, bf16[384,8192]{1,0:T(8,128)(2,1)} %bitcast.28, bf16[384,768]{1,0:T(8,128)(2,1)} %get-tuple-element.36.refs_2_, bf16[384,1536]{1,0:T(8,128)(2,1)} %get-tuple-element.37.refs_3_), custom_call_target="tpu_custom_call" | custom-call | flops 3623878656 | bytes 16777216 | tf_op jit(solution)/shard_map/sibling_grads/pallas_call | solution.py:268
  128.8 0.0 collective-permute-start.4
  128.8 0.5 collective-permute-start.5
  129.3 0.1 collective-permute-start.6
  129.3 0.0 copy-done.5
  129.3 30.6 %all_to_all.35 = bf16[16,24,2560]{2,1,0:T(8,128)(2,1)S(1)} all-to-all(bf16[16,24,2560]{2,1,0:T(8,128)(2,1)S(1)} %bitcast.33), channel_id=1, replica_groups=mesh['section'=4,'chip'=16,'core'=2] {'chip'}, dimensions={0} | all-to-all | bytes 3932160 | tf_op jit(solution)/shard_map/all_to_all | solution.py:28
  160.0 3.7 %all-to-all-start.2 = ((bf16[16,24,1536]{2,1,0:T(8,128)(2,1)}), bf16[16,24,1536]{2,1,0:T(8,128)(2,1)S(1)}, u32[]{:S(2)}, u32[]{:S(2)}) async-start(bf16[16,24,1536]{2,1,0:T(8,128)(2,1)} %bitcast.34), calls=%async_computation.2 | async-start | bytes 2359296 | tf_op jit(solution)/shard_map/all_to_all | solution.py:28
  163.7 0.0 copy-done
  163.7 1.3 convolution_convert_fusion
  165.0 0.8 collective-permute-start.3
  165.8 0.0 collective-permute-done.4.refs_4_
  165.8 0.0 collective-permute-done.5.refs_5_
  165.9 0.0 collective-permute-done.6.refs_6_
  165.9 13.6 %own_grads.1 = (bf16[4096,384]{1,0:T(8,128)(2,1)}, bf16[4096,384]{1,0:T(8,128)(2,1)}, bf16[384,4096]{1,0:T(8,128)(2,1)}) custom-call(bf16[384,8192]{1,0:T(8,128)(2,1)} %bitcast.29, bf16[384,8192]{1,0:T(8,128)(2,1)} %bitcast.30, bf16[384,768]{1,0:T(8,128)(2,1)} %get-tuple-element.36.refs_2_, bf16[384,1536]{1,0:T(8,128)(2,1)} %get-tuple-element.37.refs_3_, ...), custom_call_target="tpu_custom_call" | custom-call | flops 3623878656 | bytes 16777216 | tf_op jit(solution)/shard_map/own_grads/pallas_call | solution.py:268
  179.4 0.7 slice.3
  180.1 0.0 collective-permute-start.7
  180.1 2.1 %all-to-all-done.2 = bf16[16,24,1536]{2,1,0:T(8,128)(2,1)S(1)} async-done(((bf16[16,24,1536]{2,1,0:T(8,128)(2,1)}), bf16[16,24,1536]{2,1,0:T(8,128)(2,1)S(1)}, u32[]{:S(2)}, u32[]{:S(2)}) %all-to-all-start.2) | async-done | bytes 1179680 | tf_op jit(solution)/shard_map/all_to_all | solution.py:28
  182.2 0.0 copy-start.4
  182.2 0.0 collective-permute-done.7.mark
  182.2 0.0 copy-start.6
  182.3 1.0 copy-done.4
  183.3 0.0 copy-done.6
  183.3 3.2 %combine.1 = bf16[128,1536]{1,0:T(8,128)(2,1)} custom-call(bf16[128,384]{1,0:T(8,128)(2,1)} %copy-done, bf16[384,1536]{1,0:T(8,128)(2,1)} %bitcast.32, bf16[16,128]{1,0:T(8,128)(2,1)} %copy-done.6), custom_call_target="tpu_custom_call" | custom-call | flops 150994944 | bytes 1179648 | tf_op jit(solution)/shard_map/combine/pallas_call | solution.py:230
  186.5 0.8 collective-permute-start.8
  187.3 0.0 collective-permute-done.3
  187.3 10.4 %collective-permute-done.8 = bf16[128,1536]{1,0:T(8,128)(2,1)S(1)} collective-permute-done((bf16[128,1536]{1,0:T(8,128)(2,1)}, bf16[128,1536]{1,0:T(8,128)(2,1)S(1)}, u32[]{:S(2)}, u32[]{:S(2)}) %collective-permute-start.8) | collective-permute-done | bytes 393248 | tf_op jit(solution)/shard_map/ppermute | solution.py:308
  197.7 1.1 maximum_bitcast_fusion
Async XLA Ops:
  0.6 9.7 %collective-permute-start = (bf16[4096,384]{1,0:T(8,128)(2,1)}, bf16[4096,384]{1,0:T(8,128)(2,1)S(1)}, u32[]{:S(2)}, u32[]{:S(2)}) collective-permute-start(bf16[4096,384]{1,0:T(8,128)(2,1)} %bitcast.37), channel_id=1, source_target_pairs={{0,1},{1,0},{2,3},{3,2},{4,5},{5,4},{6,7},{7,6},{8,9},{9,8},{10,11... | collective-permute-start | bytes 9437192 | tf_op jit(solution)/shard_map/ppermute | solution.py:24
  0.7 10.5 %collective-permute-start.1 = (bf16[4096,384]{1,0:T(8,128)(2,1)}, bf16[4096,384]{1,0:T(8,128)(2,1)}, u32[]{:S(2)}, u32[]{:S(2)}) collective-permute-start(bf16[4096,384]{1,0:T(8,128)(2,1)} %bitcast.39), channel_id=1, source_target_pairs={{0,1},{1,0},{2,3},{3,2},{4,5},{5,4},{6,7},{7,6},{8,9},{9,8},{10,11... | collective-permute-start | bytes 9437192 | tf_op jit(solution)/shard_map/ppermute | solution.py:24
  1.2 14.5 %collective-permute-start.2 = (bf16[384,4096]{1,0:T(8,128)(2,1)}, bf16[384,4096]{1,0:T(8,128)(2,1)}, u32[]{:S(2)}, u32[]{:S(2)}) collective-permute-start(bf16[384,4096]{1,0:T(8,128)(2,1)} %bitcast.41), channel_id=1, source_target_pairs={{0,1},{1,0},{2,3},{3,2},{4,5},{5,4},{6,7},{7,6},{8,9},{9,8},{10,11... | collective-permute-start | bytes 9437192 | tf_op jit(solution)/shard_map/ppermute | solution.py:24
  2.8 0.7 copy-start.1
  3.5 1.2 copy-start.2
  4.7 1.2 copy-start.3
  10.3 153.4 %copy-start = (bf16[128,384]{1,0:T(8,128)(2,1)}, bf16[128,384]{1,0:T(8,128)(2,1)S(1)}, u32[]{:S(2)}) copy-start(bf16[128,384]{1,0:T(8,128)(2,1)S(1)} %get-tuple-element.30.place_back) | copy-start | bytes 294916
  10.3 87.0 %copy-start.7 = (bf16[4096,384]{1,0:T(8,128)(2,1)}, bf16[4096,384]{1,0:T(8,128)(2,1)S(1)}, u32[]{:S(2)}) copy-start(bf16[4096,384]{1,0:T(8,128)(2,1)S(1)} %collective-permute-done.gs) | copy-start | bytes 9437188
  117.8 11.5 %copy-start.5 = (bf16[384,2560]{1,0:T(8,128)(2,1)S(1)}, bf16[384,2560]{1,0:T(8,128)(2,1)}, u32[]{:S(2)}) copy-start(bf16[384,2560]{1,0:T(8,128)(2,1)} %get-tuple-element.32) | copy-start | bytes 5898244
  128.8 37.1 %collective-permute-start.4 = (bf16[4096,384]{1,0:T(8,128)(2,1)}, bf16[4096,384]{1,0:T(8,128)(2,1)}, u32[]{:S(2)}, u32[]{:S(2)}) collective-permute-start(bf16[4096,384]{1,0:T(8,128)(2,1)} %get-tuple-element.38), channel_id=1, source_target_pairs={{0,1},{1,0},{2,3},{3,2},{4,5},{5,4},{6,7},{7,6},{8,9},{9,8},{10,11... | collective-permute-start | bytes 9437192 | tf_op jit(solution)/shard_map/ppermute | solution.py:24
  128.8 37.1 %collective-permute-start.5 = (bf16[4096,384]{1,0:T(8,128)(2,1)}, bf16[4096,384]{1,0:T(8,128)(2,1)}, u32[]{:S(2)}, u32[]{:S(2)}) collective-permute-start(bf16[4096,384]{1,0:T(8,128)(2,1)} %get-tuple-element.39), channel_id=1, source_target_pairs={{0,1},{1,0},{2,3},{3,2},{4,5},{5,4},{6,7},{7,6},{8,9},{9,8},{10,11... | collective-permute-start | bytes 9437192 | tf_op jit(solution)/shard_map/ppermute | solution.py:24
  129.3 36.6 %collective-permute-start.6 = (bf16[384,4096]{1,0:T(8,128)(2,1)}, bf16[384,4096]{1,0:T(8,128)(2,1)}, u32[]{:S(2)}, u32[]{:S(2)}) collective-permute-start(bf16[384,4096]{1,0:T(8,128)(2,1)} %get-tuple-element.40), channel_id=1, source_target_pairs={{0,1},{1,0},{2,3},{3,2},{4,5},{5,4},{6,7},{7,6},{8,9},{9,8},{10,11... | collective-permute-start | bytes 9437192 | tf_op jit(solution)/shard_map/ppermute | solution.py:24
  160.0 22.3 %all-to-all-start.2 = ((bf16[16,24,1536]{2,1,0:T(8,128)(2,1)}), bf16[16,24,1536]{2,1,0:T(8,128)(2,1)S(1)}, u32[]{:S(2)}, u32[]{:S(2)}) async-start(bf16[16,24,1536]{2,1,0:T(8,128)(2,1)} %bitcast.34), calls=%async_computation.2 | async-start | bytes 2359296 | tf_op jit(solution)/shard_map/all_to_all | solution.py:28
  165.0 22.2 %collective-permute-start.3 = (bf16[128,2560]{1,0:T(8,128)(2,1)}, bf16[128,2560]{1,0:T(8,128)(2,1)S(1)}, u32[]{:S(2)}, u32[]{:S(2)}) collective-permute-start(bf16[128,2560]{1,0:T(8,128)(2,1)} %convolution_convert_fusion), channel_id=1, source_target_pairs={{0,96},{32,0},{64,32},{96,64},{1,97},{33,1},{65,33},{97,65},{2,98}... | collective-permute-start | bytes 1966088 | tf_op jit(solution)/shard_map/ppermute | solution.py:308
  180.1 2.1 %collective-permute-start.7 = (bf16[16,128]{1,0:T(8,128)(2,1)S(1)}, bf16[16,128]{1,0:T(8,128)(2,1)S(1)}, u32[]{:S(2)}, u32[]{:S(2)}) collective-permute-start(bf16[16,128]{1,0:T(8,128)(2,1)S(1)} %slice.3), channel_id=1, source_target_pairs={{0,1},{1,0},{2,3},{3,2},{4,5},{5,4},{6,7},{7,6},{8,9},{9,8},{10,11... | collective-permute-start | bytes 12296 | tf_op jit(solution)/shard_map/ppermute | solution.py:24
  182.2 1.0 copy-start.4
  182.2 1.0 copy-start.6
  186.5 11.2 %collective-permute-start.8 = (bf16[128,1536]{1,0:T(8,128)(2,1)}, bf16[128,1536]{1,0:T(8,128)(2,1)S(1)}, u32[]{:S(2)}, u32[]{:S(2)}) collective-permute-start(bf16[128,1536]{1,0:T(8,128)(2,1)} %combine.1), channel_id=1, source_target_pairs={{0,96},{32,0},{64,32},{96,64},{1,97},{33,1},{65,33},{97,65},{2,98}... | collective-permute-start | bytes 1179656 | tf_op jit(solution)/shard_map/ppermute | solution.py:308

commit v6 on v3

--- a/solution.py
+++ b/solution.py
@@ -11,7 +11,7 @@
 CORES = 2
 HALVES = SPLIT // CORES
 MIB = 1 << 20
-LIMIT = 56 * MIB
+LIMIT = 32 * MIB
 NEXT_LAST = (((1,), (1,)), ((), ()))
 FIRST_FIRST = (((0,), (0,)), ((), ()))
 
@@ -102,7 +102,7 @@
         out_shape=[jax.ShapeDtypeStruct((count, 2 * width), jnp.bfloat16) for count in slots]
         + [jax.ShapeDtypeStruct((tokens, count), jnp.bfloat16) for count in slots],
         scratch_shapes=[pltpu.VMEM((count, tokens), jnp.bfloat16) for count in slots],
-        compiler_params=pltpu.CompilerParams(vmem_limit_bytes=16 * MIB),
+        compiler_params=pltpu.CompilerParams(vmem_limit_bytes=24 * MIB),
         cost_estimate=cost(4 * sum(slots) * tokens * width, 6 * sum(slots) * width),
         name="deal_rows",
     )(ids.reshape(1, tokens), ids, gates, stash, out_grad)
@@ -212,7 +212,7 @@
             pltpu.SemaphoreType.DMA((8, steps)),
             pltpu.SemaphoreType.DMA((steps,)),
         ],
-        compiler_params=pltpu.CompilerParams(vmem_limit_bytes=40 * MIB),
+        compiler_params=pltpu.CompilerParams(vmem_limit_bytes=52 * MIB),
         cost_estimate=cost(10 * count * width * CORES * units, 30 * MIB),
         name="middle",
     )(rows, *own, *sibling)
@@ -293,7 +293,6 @@
     first = move(first)
     grads = weight_grads([rows], [hidden], [deltas], 0, received)
     last, move = shift(last)
-    last, grads = lax.optimization_barrier((last, tuple(grads)))
     last = move(last)
     prev_grad = jnp.concatenate([first, last], axis=1)
     return (prev_grad[None],) + tuple(grad[None, None] for grad in grads)

time: 196 us -> 192 us (0.980); the launches traced: 196 us -> 189 us
  waiting for transfers between devices: 46 us -> 37.6 us
  Pallas kernels: 47.7 us -> 43.9 us
  local copies, waits for them, and re-layouts: 6.49 us -> 10.2 us
    ppermute x2, waiting for transfers between devices: 6.85 us -> 0.01 us  [shift(): lax.ppermute(value, 'section', [(i, (i - 1) % sections) for i in range(se...]
    pallas_call x2, Pallas kernels: 24.4 us -> 19.3 us  [weight_grads(): pl.pallas_call(functools.partial(grads_kernel, len(rows), len(received) >...]
    unnamed x18 -> x12, local copies, waits for them, and re-layouts: 4.97 us -> 8.66 us
  transfers between devices with their start and end apart: 10 -> 10, of which waited for: 5 -> 4; matrix products, arithmetic and copies ran while one was open for 2% -> 3% of each run, Pallas kernels for 15% -> 12%
where the time goes in v6:
time: 192 us; the launch traced here: 189 us
  blocking collectives  81.6 us (42%)
  Pallas kernels  43.9 us (23%)
  waiting for transfers between devices  37.6 us (20%)
  starting transfers between devices  11 us (6%)
  local copies, waits for them, and re-layouts  10.2 us (5%)
  matrix products  3.43 us (2%)
    all_to_all x1, blocking collectives, over_chips(): lax.all_to_all(value, 'chip', split_axis=0, concat_axis=0, tiled=True)  81.6 us
    all_to_all x2, waiting for transfers between devices, over_chips(): lax.all_to_all(value, 'chip', split_axis=0, concat_axis=0, tiled=True)  32.2 us
    pallas_call x1, Pallas kernels, middle(): pl.pallas_call(functools.partial(middle_kernel, steps, cuts), in_specs=[a...  20.3 us
    pallas_call x2, Pallas kernels, weight_grads(): pl.pallas_call(functools.partial(grads_kernel, len(rows), len(received) >...  19.3 us
    unnamed x12, local copies, waits for them, and re-layouts  8.66 us
    all_to_all x2, starting transfers between devices, over_chips(): lax.all_to_all(value, 'chip', split_axis=0, concat_axis=0, tiled=True)  8.2 us
    ppermute x6, waiting for transfers between devices, swap_cores(): return lax.ppermute(value, 'core', [(0, 1), (1, 0)])  5.42 us
    pallas_call x1, Pallas kernels, deal(): pl.pallas_call(functools.partial(deal_kernel, experts, chunks, blocks), g...  4.34 us
  transfers between devices with their start and end apart: 10, of which 4 were waited for; matrix products, arithmetic and copies ran while one was open for 3% of the time, Pallas kernels for 12%

profile of v6, /device:TPU:6, one launch (start us, length us, event | category | flops | bytes accessed | tf_op | source)
XLA Modules:
  0.0 189.4 jit_solution(4638388212235970061)
XLA Ops:
  0.6 0.1 collective-permute-start
  0.7 0.5 collective-permute-start.1
  1.2 0.1 collective-permute-start.2
  1.3 0.8 copy.12.gates
  2.1 0.8 copy.11.col_ids
  2.8 0.0 copy-start.3
  2.8 0.6 copy-done.3
  3.5 0.0 copy-start.4
  3.5 1.2 copy-done.4
  4.7 0.0 copy-start.5
  4.7 1.2 copy-done.5
  5.9 4.3 %deal_rows.1 = (bf16[384,8192]{1,0:T(8,128)(2,1)S(1)}, bf16[128,384]{1,0:T(8,128)(2,1)S(1)}) custom-call(s32[1,128]{1,0:T(1,128)S(1)} %bitcast.30, s32[128,1]{1,0:T(8,128)S(1)} %copy.11.col_ids, f32[128,1]{1,0:T(8,128)S(1)} %copy.12.gates, bf16[128,4096]{1,0:T(8,128)(2,1)S(1)} %bitcast.31, bf16[128,4096]{1,0:T(8,128)(2,1)S(1)} %bitcast.32), custom_call_target="tpu_custom_call" | custom-call | flops 805306368 | bytes 9437184 | tf_op jit(solution)/shard_map/deal_rows/pallas_call | solution.py:90
  10.3 0.0 collective-permute-done.gs
  10.3 0.9 collective-permute-done.1.us
  11.2 4.5 %collective-permute-done.2.ds = bf16[384,4096]{1,0:T(8,128)(2,1)} collective-permute-done((bf16[384,4096]{1,0:T(8,128)(2,1)}, bf16[384,4096]{1,0:T(8,128)(2,1)}, u32[]{:S(2)}, u32[]{:S(2)}) %collective-permute-start.2) | collective-permute-done | bytes 3145760 | tf_op jit(solution)/shard_map/ppermute | solution.py:24
  15.7 81.6 %all_to_all.35 = bf16[16,24,8192]{2,1,0:T(8,128)(2,1)} all-to-all(bf16[16,24,8192]{2,1,0:T(8,128)(2,1)S(1)} %bitcast.28), channel_id=1, replica_groups=mesh['section'=4,'chip'=16,'core'=2] {'chip'}, dimensions={0} | all-to-all | bytes 12582912 | tf_op jit(solution)/shard_map/all_to_all | solution.py:28
  97.3 20.3 %middle.1 = (bf16[384,3072]{1,0:T(8,128)(2,1)}, bf16[384,1024]{1,0:T(8,128)(2,1)}, bf16[384,768]{1,0:T(8,128)(2,1)S(1)}, bf16[384,1536]{1,0:T(8,128)(2,1)}) custom-call(bf16[384,8192]{1,0:T(8,128)(2,1)} %bitcast.23, bf16[4096,384]{1,0:T(8,128)(2,1)} %bitcast.37, bf16[4096,384]{1,0:T(8,128)(2,1)} %bitcast.39, bf16[384,4096]{1,0:T(8,128)(2,1)} %bitcast.41, ...), custom_call_target="tpu_custom_call" | custom-call | flops 12079595520 | bytes 31457280 | tf_op jit(solution)/shard_map/middle/pallas_call | solution.py:196
  117.6 0.0 copy-start.2
  117.6 4.6 %all-to-all-start.1 = ((bf16[16,24,3072]{2,1,0:T(8,128)(2,1)}), bf16[16,24,3072]{2,1,0:T(8,128)(2,1)}, u32[]{:S(2)}, u32[]{:S(2)}) async-start(bf16[16,24,3072]{2,1,0:T(8,128)(2,1)} %bitcast.34), calls=%async_computation.1 | async-start | bytes 4718592 | tf_op jit(solution)/shard_map/all_to_all | solution.py:28
  122.2 0.0 copy-done.2
  122.2 0.0 copy-start
  122.2 2.8 %copy-done = bf16[16,24,8192]{2,1,0:T(8,128)(2,1)S(1)} copy-done((bf16[16,24,8192]{2,1,0:T(8,128)(2,1)S(1)}, bf16[16,24,8192]{2,1,0:T(8,128)(2,1)}, u32[]{:S(2)}) %copy-start) | copy-done | bytes 6291480
  125.0 8.2 %sibling_grads.1 = (bf16[4096,384]{1,0:T(8,128)(2,1)}, bf16[4096,384]{1,0:T(8,128)(2,1)}, bf16[384,4096]{1,0:T(8,128)(2,1)}) custom-call(bf16[384,8192]{1,0:T(8,128)(2,1)S(1)} %bitcast.24, bf16[384,8192]{1,0:T(8,128)(2,1)S(1)} %bitcast.25, bf16[384,768]{1,0:T(8,128)(2,1)S(1)} %get-tuple-element.36.refs_2_, bf16[384,1536]{1,0:T(8,128)(2,1)S(1)} %copy-done.2), custom_call_target="tpu_custom_call" | custom-call | flops 3623878656 | bytes 16777216 | tf_op jit(solution)/shard_map/sibling_grads/pallas_call | solution.py:244
  133.1 0.0 collective-permute-start.5
  133.1 0.5 collective-permute-start.6
  133.6 0.0 collective-permute-start.7
  133.6 21.9 %all-to-all-done.1 = bf16[16,24,3072]{2,1,0:T(8,128)(2,1)} async-done(((bf16[16,24,3072]{2,1,0:T(8,128)(2,1)}), bf16[16,24,3072]{2,1,0:T(8,128)(2,1)}, u32[]{:S(2)}, u32[]{:S(2)}) %all-to-all-start.1) | async-done | bytes 2359328 | tf_op jit(solution)/shard_map/all_to_all | solution.py:28
  155.5 3.6 %all-to-all-start.2 = ((bf16[16,24,1024]{2,1,0:T(8,128)(2,1)}), bf16[16,24,1024]{2,1,0:T(8,128)(2,1)S(1)}, u32[]{:S(2)}, u32[]{:S(2)}) async-start(bf16[16,24,1024]{2,1,0:T(8,128)(2,1)} %bitcast.12), calls=%async_computation.2 | async-start | bytes 1572864 | tf_op jit(solution)/shard_map/all_to_all | solution.py:28
  159.1 3.1 %convolution_convert_fusion = bf16[128,3072]{1,0:T(8,128)(2,1)} fusion(bf16[128,384]{1,0:T(8,128)(2,1)S(1)} %get-tuple-element.30, bf16[384,3072]{1,0:T(8,128)(2,1)} %bitcast.11), kind=kOutput, calls=%fused_computation | convolution fusion | flops 302383104 | bytes 3244032 | tf_op jit(solution)/shard_map/dot_general | solution.py:20
  162.3 0.8 collective-permute-start.3
  163.0 10.3 %all-to-all-done.2 = bf16[16,24,1024]{2,1,0:T(8,128)(2,1)S(1)} async-done(((bf16[16,24,1024]{2,1,0:T(8,128)(2,1)}), bf16[16,24,1024]{2,1,0:T(8,128)(2,1)S(1)}, u32[]{:S(2)}, u32[]{:S(2)}) %all-to-all-start.2) | async-done | bytes 786464 | tf_op jit(solution)/shard_map/all_to_all | solution.py:28
  173.3 0.3 convolution_convert_fusion.1
  173.6 0.8 collective-permute-start.4
  174.4 0.0 collective-permute-done.5.refs_4_
  174.4 0.0 collective-permute-done.6.refs_5_
  174.5 0.0 collective-permute-done.7.refs_6_
  174.5 0.0 copy-start.1
  174.5 2.8 %copy-done.1 = bf16[16,24,8192]{2,1,0:T(8,128)(2,1)S(1)} copy-done((bf16[16,24,8192]{2,1,0:T(8,128)(2,1)S(1)}, bf16[16,24,8192]{2,1,0:T(8,128)(2,1)}, u32[]{:S(2)}) %copy-start.1) | copy-done | bytes 6291480
  177.2 11.1 %own_grads.1 = (bf16[4096,384]{1,0:T(8,128)(2,1)}, bf16[4096,384]{1,0:T(8,128)(2,1)}, bf16[384,4096]{1,0:T(8,128)(2,1)}) custom-call(bf16[384,8192]{1,0:T(8,128)(2,1)S(1)} %bitcast.26, bf16[384,8192]{1,0:T(8,128)(2,1)S(1)} %bitcast.27, bf16[384,768]{1,0:T(8,128)(2,1)S(1)} %get-tuple-element.36.refs_2_, bf16[384,1536]{1,0:T(8,128)(2,1)S(1)} %copy-done.2, ...), custom_call_target="tpu_custom_call" | custom-call | flops 3623878656 | bytes 16777216 | tf_op jit(solution)/shard_map/own_grads/pallas_call | solution.py:244
  188.4 0.0 collective-permute-done.3
  188.4 0.0 collective-permute-done.4
  188.4 1.0 maximum_bitcast_fusion
Async XLA Ops:
  0.6 9.7 %collective-permute-start = (bf16[4096,384]{1,0:T(8,128)(2,1)}, bf16[4096,384]{1,0:T(8,128)(2,1)}, u32[]{:S(2)}, u32[]{:S(2)}) collective-permute-start(bf16[4096,384]{1,0:T(8,128)(2,1)} %bitcast.36), channel_id=1, source_target_pairs={{0,1},{1,0},{2,3},{3,2},{4,5},{5,4},{6,7},{7,6},{8,9},{9,8},{10,11... | collective-permute-start | bytes 9437192 | tf_op jit(solution)/shard_map/ppermute | solution.py:24
  0.7 10.5 %collective-permute-start.1 = (bf16[4096,384]{1,0:T(8,128)(2,1)}, bf16[4096,384]{1,0:T(8,128)(2,1)}, u32[]{:S(2)}, u32[]{:S(2)}) collective-permute-start(bf16[4096,384]{1,0:T(8,128)(2,1)} %bitcast.38), channel_id=1, source_target_pairs={{0,1},{1,0},{2,3},{3,2},{4,5},{5,4},{6,7},{7,6},{8,9},{9,8},{10,11... | collective-permute-start | bytes 9437192 | tf_op jit(solution)/shard_map/ppermute | solution.py:24
  1.2 14.5 %collective-permute-start.2 = (bf16[384,4096]{1,0:T(8,128)(2,1)}, bf16[384,4096]{1,0:T(8,128)(2,1)}, u32[]{:S(2)}, u32[]{:S(2)}) collective-permute-start(bf16[384,4096]{1,0:T(8,128)(2,1)} %bitcast.40), channel_id=1, source_target_pairs={{0,1},{1,0},{2,3},{3,2},{4,5},{5,4},{6,7},{7,6},{8,9},{9,8},{10,11... | collective-permute-start | bytes 9437192 | tf_op jit(solution)/shard_map/ppermute | solution.py:24
  2.8 0.7 copy-start.3
  3.5 1.2 copy-start.4
  4.7 1.2 copy-start.5
  117.6 4.6 %copy-start.2 = (bf16[384,1536]{1,0:T(8,128)(2,1)S(1)}, bf16[384,1536]{1,0:T(8,128)(2,1)}, u32[]{:S(2)}) copy-start(bf16[384,1536]{1,0:T(8,128)(2,1)} %get-tuple-element.37.refs_3_) | copy-start | bytes 3538948
  117.6 37.9 %all-to-all-start.1 = ((bf16[16,24,3072]{2,1,0:T(8,128)(2,1)}), bf16[16,24,3072]{2,1,0:T(8,128)(2,1)}, u32[]{:S(2)}, u32[]{:S(2)}) async-start(bf16[16,24,3072]{2,1,0:T(8,128)(2,1)} %bitcast.34), calls=%async_computation.1 | async-start | bytes 4718592 | tf_op jit(solution)/shard_map/all_to_all | solution.py:28
  122.2 2.8 %copy-start = (bf16[16,24,8192]{2,1,0:T(8,128)(2,1)S(1)}, bf16[16,24,8192]{2,1,0:T(8,128)(2,1)}, u32[]{:S(2)}) copy-start(bf16[16,24,8192]{2,1,0:T(8,128)(2,1)} %all_to_all.35) | copy-start | bytes 18874372
  133.1 41.3 %collective-permute-start.5 = (bf16[4096,384]{1,0:T(8,128)(2,1)}, bf16[4096,384]{1,0:T(8,128)(2,1)}, u32[]{:S(2)}, u32[]{:S(2)}) collective-permute-start(bf16[4096,384]{1,0:T(8,128)(2,1)} %get-tuple-element.38), channel_id=1, source_target_pairs={{0,1},{1,0},{2,3},{3,2},{4,5},{5,4},{6,7},{7,6},{8,9},{9,8},{10,11... | collective-permute-start | bytes 9437192 | tf_op jit(solution)/shard_map/ppermute | solution.py:24
  133.1 41.3 %collective-permute-start.6 = (bf16[4096,384]{1,0:T(8,128)(2,1)}, bf16[4096,384]{1,0:T(8,128)(2,1)}, u32[]{:S(2)}, u32[]{:S(2)}) collective-permute-start(bf16[4096,384]{1,0:T(8,128)(2,1)} %get-tuple-element.39), channel_id=1, source_target_pairs={{0,1},{1,0},{2,3},{3,2},{4,5},{5,4},{6,7},{7,6},{8,9},{9,8},{10,11... | collective-permute-start | bytes 9437192 | tf_op jit(solution)/shard_map/ppermute | solution.py:24
  133.6 40.8 %collective-permute-start.7 = (bf16[384,4096]{1,0:T(8,128)(2,1)}, bf16[384,4096]{1,0:T(8,128)(2,1)}, u32[]{:S(2)}, u32[]{:S(2)}) collective-permute-start(bf16[384,4096]{1,0:T(8,128)(2,1)} %get-tuple-element.40), channel_id=1, source_target_pairs={{0,1},{1,0},{2,3},{3,2},{4,5},{5,4},{6,7},{7,6},{8,9},{9,8},{10,11... | collective-permute-start | bytes 9437192 | tf_op jit(solution)/shard_map/ppermute | solution.py:24
  155.5 17.8 %all-to-all-start.2 = ((bf16[16,24,1024]{2,1,0:T(8,128)(2,1)}), bf16[16,24,1024]{2,1,0:T(8,128)(2,1)S(1)}, u32[]{:S(2)}, u32[]{:S(2)}) async-start(bf16[16,24,1024]{2,1,0:T(8,128)(2,1)} %bitcast.12), calls=%async_computation.2 | async-start | bytes 1572864 | tf_op jit(solution)/shard_map/all_to_all | solution.py:28
  162.3 26.1 %collective-permute-start.3 = (bf16[128,3072]{1,0:T(8,128)(2,1)}, bf16[128,3072]{1,0:T(8,128)(2,1)S(1)}, u32[]{:S(2)}, u32[]{:S(2)}) collective-permute-start(bf16[128,3072]{1,0:T(8,128)(2,1)} %convolution_convert_fusion), channel_id=1, source_target_pairs={{0,96},{32,0},{64,32},{96,64},{1,97},{33,1},{65,33},{97,65},{2,98}... | collective-permute-start | bytes 2359304 | tf_op jit(solution)/shard_map/ppermute | solution.py:284
  173.6 14.7 %collective-permute-start.4 = (bf16[128,1024]{1,0:T(8,128)(2,1)S(1)}, bf16[128,1024]{1,0:T(8,128)(2,1)S(1)}, u32[]{:S(2)}, u32[]{:S(2)}) collective-permute-start(bf16[128,1024]{1,0:T(8,128)(2,1)S(1)} %convolution_convert_fusion.1), channel_id=1, source_target_pairs={{0,96},{32,0},{64,32},{96,64},{1,97},{33,1},{65,33},{97,65},{2,98}... | collective-permute-start | bytes 786440 | tf_op jit(solution)/shard_map/ppermute | solution.py:284
  174.5 2.8 %copy-start.1 = (bf16[16,24,8192]{2,1,0:T(8,128)(2,1)S(1)}, bf16[16,24,8192]{2,1,0:T(8,128)(2,1)}, u32[]{:S(2)}) copy-start(bf16[16,24,8192]{2,1,0:T(8,128)(2,1)} %all_to_all.35) | copy-start | bytes 18874372
